TPU v7x, 32 devices: a whole 2x2x4 slice. The times are simulated.
32 devices in a mesh: space: 4 (over z), bal: 8 (over y, x, core).
Axes of the slice: x: 2, y: 2, z: 4, core: 2. Of those that a mesh axis runs over, the one named last changes fastest.
Arguments:
- panels: bfloat16 [4, 8, 1024, 1024], P('space', 'bal'), may hold values from -0.1875 to 0.1875
- enrich: int32 [4, 8], P('space', 'bal'), may hold values from 1 to 2
- compliance: float32 [4, 8, 1024], P('space', 'bal'), may hold values from 0.5 to 2
- loads: float32 [4, 8, 64, 1024], P('space', 'bal'), may hold values from -6 to 6
- face_maps: int32 [4, 8, 4, 256], P('space', 'bal'), may hold values from 0 to 255, each once within a row
- face_lengths: int32 [4, 8, 4], P('space', 'bal'), may hold values from 128 to 256, as said below
- contact: int32 [4, 8, 128], P('space', 'bal'), may hold values from 0 to 1023
Outputs:
- solution: float32 [4, 8, 64, 1024], P('space', 'bal')
- residual: float32 [4, 8, 64, 1024], P('space', 'bal')
- violation: float32 [64], replicated
Inputs may be any that keep to these rules, and one draw needn't show every extreme that they name: `face_maps`: each face's slot-to-row table is a permutation of its 256 rows. `face_lengths`: the two faces of one shared interface have the same length; some face has all 256 slots live.
All inputs are finite; a program needn't handle non-finite values.
Results may differ from a plain program's by a relative error of at most 0.0003.
Values sent between devices are 32-bit elements; how exact they have to be, the bound alone decides.
A program may use at most 64 MiB of HBM per device.

v0:
```python
import math

import jax
import jax.numpy as jnp
from jax import lax
from jax.sharding import PartitionSpec as P

IFACE = 1024
ROWS = 1024
BLOCK_ROWS = 512
ITERS = 3


def padded(block, sides, width):
    for axis, dim in sides:
        count = lax.axis_size(axis)
        forward = [(i, i + 1) for i in range(count - 1)]
        backward = [(target, source) for source, target in forward]
        low = lax.ppermute(
            lax.slice_in_dim(block, block.shape[dim] - width, None, axis=dim), axis, forward
        )
        high = lax.ppermute(lax.slice_in_dim(block, 0, width, axis=dim), axis, backward)
        block = jnp.concatenate([low, block, high], axis=dim)
    return block


def chebyshev_constants():
    upper = 2.6 * (1.0 + math.sqrt(IFACE / ROWS)) ** 2 + 4.0
    lower = 0.5
    center = (upper + lower) / 2.0
    half_span = (upper - lower) / 2.0
    return (center, half_span, center / half_span)


def canon_order(field, position):
    picked = jnp.take(field, position, axis=1)
    return jnp.moveaxis(picked, 1, 0)


def local_order(summed, inverse):
    face_rows = jnp.take_along_axis(summed, inverse[:, None, :], axis=2)
    return jnp.moveaxis(face_rows, 0, 1).reshape(summed.shape[1], -1)


def assemble(field, position, inverse):
    canonical = canon_order(field, position)
    along_space = padded(canonical[0:2], (("space", 0),), 1)
    along_bal = padded(canonical[2:4], (("bal", 0),), 1)
    outside = (along_space[0], along_space[3], along_bal[0], along_bal[3])
    summed = jnp.stack([canonical[side_index] + outside[side_index] for side_index in range(4)])
    return local_order(summed, inverse)


def local(panels, enrich, compliance, loads, face_maps, face_lengths, contact):
    panel_rows = panels[0, 0]
    columns = panel_rows.shape[1]
    face_len = columns // 4

    def add_block(block_number, running):
        block_data = lax.dynamic_slice_in_dim(panel_rows, block_number * BLOCK_ROWS, BLOCK_ROWS, 0)
        return running + lax.dot_general(
            block_data, block_data, (((0,), (0,)), ((), ())), preferred_element_type=jnp.float32
        )

    gram_matrix = lax.fori_loop(
        0, enrich[0, 0], add_block, jnp.zeros((columns, columns), jnp.float32)
    )
    diag_terms = compliance[0, 0]
    table = face_maps[0, 0]
    canon_slot = jnp.arange(face_len, dtype=jnp.int32)
    live_canon = (canon_slot[None, :] < face_lengths[0, 0][:, None]).astype(jnp.float32)
    inverse = jnp.argsort(table, axis=1)
    live_local = jnp.take_along_axis(live_canon, inverse, axis=1).reshape(1, columns)
    position = table + (jnp.arange(4, dtype=jnp.int32) * face_len)[:, None]
    center, half_span, ratio_c = chebyshev_constants()
    residual = assemble(live_local * loads[0, 0], position, inverse)
    direction = residual / center
    solution = jnp.zeros_like(residual)
    cheb_rho = 1.0 / ratio_c
    for iteration in range(ITERS):
        solution = solution + direction
        product = jnp.dot(direction, gram_matrix, precision=lax.Precision.HIGHEST)
        residual = residual - assemble(
            live_local * (product + direction * diag_terms[None, :]), position, inverse
        )
        if iteration + 1 < ITERS:
            rho_next = 1.0 / (2.0 * ratio_c - cheb_rho)
            direction = rho_next * cheb_rho * direction + 2.0 * rho_next / half_span * residual
            cheb_rho = rho_next
    gathered = jnp.take(solution, contact[0, 0], axis=1)
    negative = jnp.minimum(gathered, 0.0)
    own_terms = jnp.sum(negative * negative, axis=1)
    summed_terms = lax.psum(own_terms, ("space", "bal"))
    violation = jnp.sqrt(summed_terms + 1e-06)
    return (solution[None, None], residual[None, None], violation)


def solution(mesh):
    in_specs = (
        P("space", "bal", None, None),
        P("space", "bal"),
        P("space", "bal", None),
        P("space", "bal", None, None),
        P("space", "bal", None, None),
        P("space", "bal", None),
        P("space", "bal", None),
    )
    out_specs = (P("space", "bal", None, None), P("space", "bal", None, None), P())
    return jax.shard_map(local, mesh=mesh, in_specs=in_specs, out_specs=out_specs, check_vma=False)
```

profile of v0, /device:TPU:0, one launch (start us, length us, event | category | flops | bytes accessed | tf_op | source)
XLA Modules:
  0.0 199.5 jit_solution(7147778739456183295)
XLA Ops:
  7.2 0.6 iota.16
  7.8 0.1 sort.19.cloned.1.call-update
  7.9 0.8 fusion.15
  8.7 0.8 compare_and_fusion
  9.4 2.5 %broadcast_in_dim.44 = f32[1024,1024]{1,0:T(8,128)} broadcast(f32[]{:T(128)} %constant.48.clone.1), dimensions={} | broadcast | bytes 4194308 | tf_op jit(solution)/shard_map/broadcast_in_dim | solution.py:66
  11.9 6.8 %while.10 = (s32[]{:T(128)}, f32[1024,1024]{1,0:T(8,128)}, s32[]{:T(128)}, bf16[1024,1024]{1,0:T(8,128)(2,1)S(1)}, s32[]{:T(128)}, /*index=5*/s32[]{:T(128)}, s32[]{:T(128)}, s32[]{:T(128)}) while((s32[]{:T(128)}, f32[1024,1024]{1,0:T(8,128)}, s32[]{:T(128)}, bf16[1024,1024]{1,0:T(8,128)(2,1)S(1)}, s32[]{:T(128)}, /*index=5*/s32[]{:T(128)}, ...), condition=%wide.region_2.5_spmd, body=%wide.region_1.4_spmd.sunk | while | flops 1074790400 | bytes 9437327 | solution.py:65
  12.6 5.4 %convolution_add_fusion.5 = f32[1024,1024]{1,0:T(8,128)} fusion(f32[1024,1024]{1,0:T(8,128)} %get-tuple-element.110, bf16[1024,1024]{1,0:T(8,128)(2,1)S(1)} %get-tuple-element.120, s32[]{:T(128)S(6)} %select_n.135), kind=kOutput, calls=%fused_computation.10.clone.1 | convolution fusion | flops 1074790400 | bytes 9437188 | tf_op jit(solution)/shard_map/while/body/dot_general | solution.py:61
  18.8 0.1 fusion.14
  18.9 0.8 fusion.12
  19.7 9.1 %gather_fusion.1 = f32[1024]{0:T(1024)S(1)} fusion(f32[4,256]{1,0:T(4,128)S(1)} %fusion.14, s32[1024]{0:T(1024)S(1)} %bitcast.134), kind=kCustom, calls=%fused_computation.9 | custom fusion | bytes 16384 | tf_op jit(solution)/shard_map/jit(take_along_axis)/gather | solution.py:73
  28.9 0.2 copy.19
  29.1 2.8 %gather_fusion.2 = f32[1024,64]{1,0:T(8,128)S(1)} fusion(f32[64,1024]{0,1:T(8,128)S(1)} %copy.19, s32[1024]{0:T(1024)S(1)} %broadcast_clamp_fusion), kind=kCustom, calls=%fused_computation.clone | custom fusion | bytes 528384 | tf_op jit(solution)/shard_map/jit(_take)/gather | solution.py:36
  31.9 0.2 select_bitcast_fusion.3
  32.2 4.9 %collective-permute-start = (f32[1,64,256]{1,2,0:T(8,128)S(1)}, f32[1,64,256]{1,2,0:T(8,128)S(1)}, u32[]{:S(2)}, u32[]{:S(2)}) collective-permute-start(f32[1,64,256]{1,2,0:T(8,128)S(1)} %get-tuple-element.69), channel_id=1, source_target_pairs={{0,8},{8,16},{16,24},{1,9},{9,17},{17,25},{2,10},{10,18},{18,26},{... | collective-permute-start | bytes 196616 | tf_op jit(solution)/shard_map/ppermute | solution.py:19
  37.1 1.3 collective-permute-start.1
  38.4 4.8 %collective-permute-start.2 = (f32[1,64,256]{1,2,0:T(8,128)S(1)}, f32[1,64,256]{1,2,0:T(8,128)S(1)}, u32[]{:S(2)}, u32[]{:S(2)}) collective-permute-start(f32[1,64,256]{1,2,0:T(8,128)S(1)} %get-tuple-element.70), channel_id=1, source_target_pairs={{0,1},{1,2},{2,3},{3,4},{4,5},{5,6},{6,7},{8,9},{9,10},{10,11},{11... | collective-permute-start | bytes 196616 | tf_op jit(solution)/shard_map/ppermute | solution.py:19
  43.3 1.3 collective-permute-start.3
  44.6 5.0 %collective-permute-done.1 = f32[1,64,256]{1,2,0:T(8,128)S(1)} collective-permute-done((f32[1,64,256]{1,2,0:T(8,128)S(1)}, f32[1,64,256]{1,2,0:T(8,128)S(1)}, u32[]{:S(2)}, u32[]{:S(2)}) %collective-permute-start.1) | collective-permute-done | bytes 65568 | tf_op jit(solution)/shard_map/ppermute | solution.py:22
  49.7 1.1 collective-permute-done.3
  50.9 6.8 %gather_fusion.3 = f32[1024,64]{1,0:T(8,128)S(1)} fusion(f32[4,64,256]{1,2,0:T(8,128)S(1)} %pad_maximum_fusion, s32[1024]{0:T(1024)S(1)} %bitcast.130), kind=kCustom, calls=%fused_computation.1.clone | custom fusion | bytes 532480 | tf_op jit(solution)/shard_map/jit(take_along_axis)/gather | solution.py:41
  57.7 0.2 copy.20
  57.9 0.1 broadcast_select_fusion.2
  58.0 4.8 %fusion.4 = f32[64,1024]{1,0:T(8,128)S(1)} fusion(f32[1024,1024]{1,0:T(8,128)} %get-tuple-element.30, f32[64,1024]{1,0:T(8,128)S(1)} %bitcast.136, f32[1024]{0:T(1024)S(1)} %broadcast_multiply_fusion, f32[1024]{0:T(1024)S(1)} %bitcast.156), kind=kOutput, calls=%fused_computation.18 | convolution fusion | flops 805568512 | bytes 4726784 | tf_op jit(solution)/shard_map/dot_general | solution.py:82
  62.9 0.2 copy.21
  63.1 2.8 %gather_fusion.4 = f32[1024,64]{1,0:T(8,128)S(1)} fusion(f32[64,1024]{0,1:T(8,128)S(1)} %copy.21, s32[1024]{0:T(1024)S(1)} %broadcast_clamp_fusion), kind=kCustom, calls=%fused_computation.2.clone | custom fusion | bytes 528384 | tf_op jit(solution)/shard_map/jit(_take)/gather | solution.py:36
  65.9 0.2 select_bitcast_fusion.2
  66.2 4.6 %collective-permute-start.4 = (f32[1,64,256]{1,2,0:T(8,128)S(1)}, f32[1,64,256]{1,2,0:T(8,128)S(1)}, u32[]{:S(2)}, u32[]{:S(2)}) collective-permute-start(f32[1,64,256]{1,2,0:T(8,128)S(1)} %get-tuple-element.61), channel_id=1, source_target_pairs={{0,8},{8,16},{16,24},{1,9},{9,17},{17,25},{2,10},{10,18},{18,26},{... | collective-permute-start | bytes 196616 | tf_op jit(solution)/shard_map/ppermute | solution.py:19
  70.7 1.3 collective-permute-start.5
  72.0 5.2 %collective-permute-start.6 = (f32[1,64,256]{1,2,0:T(8,128)S(1)}, f32[1,64,256]{1,2,0:T(8,128)S(1)}, u32[]{:S(2)}, u32[]{:S(2)}) collective-permute-start(f32[1,64,256]{1,2,0:T(8,128)S(1)} %get-tuple-element.62), channel_id=1, source_target_pairs={{0,1},{1,2},{2,3},{3,4},{4,5},{5,6},{6,7},{8,9},{9,10},{10,11},{11... | collective-permute-start | bytes 196616 | tf_op jit(solution)/shard_map/ppermute | solution.py:19
  77.2 1.3 collective-permute-start.7
  78.6 1.9 collective-permute-done.7
  80.6 6.8 %gather_fusion.5 = f32[1024,64]{1,0:T(8,128)S(1)} fusion(f32[4,64,256]{1,2,0:T(8,128)S(1)} %pad_maximum_fusion.1, s32[1024]{0:T(1024)S(1)} %bitcast.131), kind=kCustom, calls=%fused_computation.5.clone | custom fusion | bytes 532480 | tf_op jit(solution)/shard_map/jit(take_along_axis)/gather | solution.py:41
  87.4 0.2 copy.22
  87.7 4.9 %fusion.3 = f32[64,1024]{1,0:T(8,128)S(1)} fusion(f32[1024,1024]{1,0:T(8,128)} %get-tuple-element.30, f32[1024]{0:T(1024)S(1)} %bitcast.160, f32[64,1024]{1,0:T(8,128)S(1)} %sub.48, f32[64,1024]{1,0:T(8,128)S(1)} %bitcast.138, f32[1024]{0:T(1024)S(1)} %bitcast.157), kind=kOutput, calls=%fused_computation.16 | convolution fusion | flops 805896192 | bytes 4988928 | tf_op jit(solution)/shard_map/dot_general | solution.py:82
  92.6 0.2 copy.23
  92.8 2.8 %gather_fusion.6 = f32[1024,64]{1,0:T(8,128)S(1)} fusion(f32[64,1024]{0,1:T(8,128)S(1)} %copy.23, s32[1024]{0:T(1024)S(1)} %broadcast_clamp_fusion), kind=kCustom, calls=%fused_computation.3.clone | custom fusion | bytes 528384 | tf_op jit(solution)/shard_map/jit(_take)/gather | solution.py:36
  95.6 0.2 select_bitcast_fusion.1
  95.9 4.3 %collective-permute-start.8 = (f32[1,64,256]{1,2,0:T(8,128)S(1)}, f32[1,64,256]{1,2,0:T(8,128)S(1)}, u32[]{:S(2)}, u32[]{:S(2)}) collective-permute-start(f32[1,64,256]{1,2,0:T(8,128)S(1)} %get-tuple-element.53), channel_id=1, source_target_pairs={{0,8},{8,16},{16,24},{1,9},{9,17},{17,25},{2,10},{10,18},{18,26},{... | collective-permute-start | bytes 196616 | tf_op jit(solution)/shard_map/ppermute | solution.py:19
  100.1 1.3 collective-permute-start.9
  101.4 5.5 %collective-permute-start.10 = (f32[1,64,256]{1,2,0:T(8,128)S(1)}, f32[1,64,256]{1,2,0:T(8,128)S(1)}, u32[]{:S(2)}, u32[]{:S(2)}) collective-permute-start(f32[1,64,256]{1,2,0:T(8,128)S(1)} %get-tuple-element.54), channel_id=1, source_target_pairs={{0,1},{1,2},{2,3},{3,4},{4,5},{5,6},{6,7},{8,9},{9,10},{10,11},{11... | collective-permute-start | bytes 196616 | tf_op jit(solution)/shard_map/ppermute | solution.py:19
  106.9 1.5 collective-permute-start.11
  108.4 1.7 collective-permute-done.11
  110.3 6.8 %gather_fusion.7 = f32[1024,64]{1,0:T(8,128)S(1)} fusion(f32[4,64,256]{1,2,0:T(8,128)S(1)} %pad_maximum_fusion.2, s32[1024]{0:T(1024)S(1)} %bitcast.132), kind=kCustom, calls=%fused_computation.6.clone | custom fusion | bytes 532480 | tf_op jit(solution)/shard_map/jit(take_along_axis)/gather | solution.py:41
  117.0 0.2 copy.24
  117.3 0.3 fusion.6
  117.6 4.9 %fusion.2 = f32[64,1024]{1,0:T(8,128)S(1)} fusion(f32[1024,1024]{1,0:T(8,128)} %get-tuple-element.30, f32[1024]{0:T(1024)S(1)} %bitcast.161, f32[64,1024]{1,0:T(8,128)S(1)} %sub.48, f32[64,1024]{1,0:T(8,128)S(1)} %bitcast.141, f32[64,1024]{1,0:T(8,128)S(1)} %bitcast.139, f32[1024]{0:T(1024)S(1)} %bitcast.158), kind=kOutput, calls=%fused_computation.14 | convolution fusion | flops 806420480 | bytes 5251072 | tf_op jit(solution)/shard_map/dot_general | solution.py:82
  122.5 0.1 add_add_fusion
  122.6 0.2 copy.25
  122.8 2.8 %gather_fusion.8 = f32[1024,64]{1,0:T(8,128)S(1)} fusion(f32[64,1024]{0,1:T(8,128)S(1)} %copy.25, s32[1024]{0:T(1024)S(1)} %broadcast_clamp_fusion), kind=kCustom, calls=%fused_computation.4.clone | custom fusion | bytes 528384 | tf_op jit(solution)/shard_map/jit(_take)/gather | solution.py:36
  125.6 0.2 select_bitcast_fusion
  125.9 4.3 %collective-permute-start.12 = (f32[1,64,256]{1,2,0:T(8,128)S(1)}, f32[1,64,256]{1,2,0:T(8,128)S(1)}, u32[]{:S(2)}, u32[]{:S(2)}) collective-permute-start(f32[1,64,256]{1,2,0:T(8,128)S(1)} %get-tuple-element.45), channel_id=1, source_target_pairs={{0,8},{8,16},{16,24},{1,9},{9,17},{17,25},{2,10},{10,18},{18,26},{... | collective-permute-start | bytes 196616 | tf_op jit(solution)/shard_map/ppermute | solution.py:19
  130.2 1.3 collective-permute-start.13
  131.5 6.0 %collective-permute-start.14 = (f32[1,64,256]{1,2,0:T(8,128)S(1)}, f32[1,64,256]{1,2,0:T(8,128)S(1)}, u32[]{:S(2)}, u32[]{:S(2)}) collective-permute-start(f32[1,64,256]{1,2,0:T(8,128)S(1)} %get-tuple-element.46), channel_id=1, source_target_pairs={{0,1},{1,2},{2,3},{3,4},{4,5},{5,6},{6,7},{8,9},{9,10},{10,11},{11... | collective-permute-start | bytes 196616 | tf_op jit(solution)/shard_map/ppermute | solution.py:19
  137.5 1.3 collective-permute-start.15
  138.8 0.2 copy.27
  139.0 0.7 gather_fusion
  139.6 0.1 multiply_reduce_fusion
  139.7 43.5 %psum.7 = f32[64]{0:T(128)S(1)} all-reduce(f32[64]{0:T(128)S(1)} %multiply_reduce_fusion), channel_id=1, replica_groups=mesh['space'=4,'bal'=8] {'space','bal'}, use_global_device_ids=true, to_apply=%region_4.7 | all-reduce | flops 64 | bytes 512 | tf_op jit(solution)/shard_map/psum | solution.py:93
  183.2 0.5 add_sqrt_fusion
  183.7 0.8 reshape.211
  184.7 6.8 %gather_fusion.9 = f32[1024,64]{1,0:T(8,128)S(1)} fusion(f32[4,64,256]{1,2,0:T(8,128)S(1)} %pad_maximum_fusion.3, s32[1024]{0:T(1024)S(1)} %bitcast.133), kind=kCustom, calls=%fused_computation.7.clone | custom fusion | bytes 532480 | tf_op jit(solution)/shard_map/jit(take_along_axis)/gather | solution.py:41
  191.5 0.2 copy.26
  191.7 0.2 bitcast_subtract_fusion
  191.9 0.8 sub.52
  (57 shorter events, 1.0 us)
Async XLA Ops:
  7.2 4.8 %copy-start = (bf16[1,1,1024,1024]{3,2,1,0:T(8,128)(2,1)S(1)}, bf16[1,1,1024,1024]{3,2,1,0:T(8,128)(2,1)}, u32[]{:S(2)}) copy-start(bf16[1,1,1024,1024]{3,2,1,0:T(8,128)(2,1)} %param.13) | copy-start | bytes 6291460
  7.2 11.7 %sort.19.cloned.1.call-start = ((), (), s32[]{:S(2)}) async-start(), calls=%async_computation | async-start | bytes 24608 | tf_op jit(solution)/shard_map/jit(argsort)/sort | solution.py:72
  11.9 6.8 %copy-start.4 = (s32[1,1,4]{2,1,0:T(1,128)S(1)}, s32[1,1,4]{2,1,0:T(1,128)}, u32[]{:S(2)}) copy-start(s32[1,1,4]{2,1,0:T(1,128)} %param.18) | copy-start | bytes 52
  11.9 6.9 %copy-start.2 = (f32[1,1,1024]{2,1,0:T(1,128)S(1)}, f32[1,1,1024]{2,1,0:T(1,128)}, u32[]{:S(2)}) copy-start(f32[1,1,1024]{2,1,0:T(1,128)} %param.15) | copy-start | bytes 12292
  11.9 6.9 %copy-start.5 = (s32[1,1,128]{2,1,0:T(1,128)S(1)}, s32[1,1,128]{2,1,0:T(1,128)}, u32[]{:S(2)}) copy-start(s32[1,1,128]{2,1,0:T(1,128)} %param.19) | copy-start | bytes 1540
  18.7 10.1 %copy-start.1 = (f32[1,1,64,1024]{3,2,1,0:T(8,128)S(1)}, f32[1,1,64,1024]{3,2,1,0:T(8,128)}, u32[]{:S(2)}) copy-start(f32[1,1,64,1024]{3,2,1,0:T(8,128)} %param.16) | copy-start | bytes 786436
  18.9 9.9 %copy-start.3 = (s32[4,256]{1,0:T(4,128)S(1)}, s32[4,256]{1,0:T(4,128)}, u32[]{:S(2)}) copy-start(s32[4,256]{1,0:T(4,128)} %get-tuple-element.29) | copy-start | bytes 12292
  32.2 12.4 %collective-permute-start = (f32[1,64,256]{1,2,0:T(8,128)S(1)}, f32[1,64,256]{1,2,0:T(8,128)S(1)}, u32[]{:S(2)}, u32[]{:S(2)}) collective-permute-start(f32[1,64,256]{1,2,0:T(8,128)S(1)} %get-tuple-element.69), channel_id=1, source_target_pairs={{0,8},{8,16},{16,24},{1,9},{9,17},{17,25},{2,10},{10,18},{18,26},{... | collective-permute-start | bytes 196616 | tf_op jit(solution)/shard_map/ppermute | solution.py:19
  37.1 12.5 %collective-permute-start.1 = (f32[1,64,256]{1,2,0:T(8,128)S(1)}, f32[1,64,256]{1,2,0:T(8,128)S(1)}, u32[]{:S(2)}, u32[]{:S(2)}) collective-permute-start(f32[1,64,256]{1,2,0:T(8,128)S(1)} %get-tuple-element.72), channel_id=1, source_target_pairs={{8,0},{16,8},{24,16},{9,1},{17,9},{25,17},{10,2},{18,10},{26,18},{... | collective-permute-start | bytes 196616 | tf_op jit(solution)/shard_map/ppermute | solution.py:22
  38.4 11.2 %collective-permute-start.2 = (f32[1,64,256]{1,2,0:T(8,128)S(1)}, f32[1,64,256]{1,2,0:T(8,128)S(1)}, u32[]{:S(2)}, u32[]{:S(2)}) collective-permute-start(f32[1,64,256]{1,2,0:T(8,128)S(1)} %get-tuple-element.70), channel_id=1, source_target_pairs={{0,1},{1,2},{2,3},{3,4},{4,5},{5,6},{6,7},{8,9},{9,10},{10,11},{11... | collective-permute-start | bytes 196616 | tf_op jit(solution)/shard_map/ppermute | solution.py:19
  43.3 7.5 %collective-permute-start.3 = (f32[1,64,256]{1,2,0:T(8,128)S(1)}, f32[1,64,256]{1,2,0:T(8,128)S(1)}, u32[]{:S(2)}, u32[]{:S(2)}) collective-permute-start(f32[1,64,256]{1,2,0:T(8,128)S(1)} %get-tuple-element.71), channel_id=1, source_target_pairs={{1,0},{2,1},{3,2},{4,3},{5,4},{6,5},{7,6},{9,8},{10,9},{11,10},{12... | collective-permute-start | bytes 196616 | tf_op jit(solution)/shard_map/ppermute | solution.py:22
  66.2 12.4 %collective-permute-start.4 = (f32[1,64,256]{1,2,0:T(8,128)S(1)}, f32[1,64,256]{1,2,0:T(8,128)S(1)}, u32[]{:S(2)}, u32[]{:S(2)}) collective-permute-start(f32[1,64,256]{1,2,0:T(8,128)S(1)} %get-tuple-element.61), channel_id=1, source_target_pairs={{0,8},{8,16},{16,24},{1,9},{9,17},{17,25},{2,10},{10,18},{18,26},{... | collective-permute-start | bytes 196616 | tf_op jit(solution)/shard_map/ppermute | solution.py:19
  70.7 7.8 %collective-permute-start.5 = (f32[1,64,256]{1,2,0:T(8,128)S(1)}, f32[1,64,256]{1,2,0:T(8,128)S(1)}, u32[]{:S(2)}, u32[]{:S(2)}) collective-permute-start(f32[1,64,256]{1,2,0:T(8,128)S(1)} %get-tuple-element.64), channel_id=1, source_target_pairs={{8,0},{16,8},{24,16},{9,1},{17,9},{25,17},{10,2},{18,10},{26,18},{... | collective-permute-start | bytes 196616 | tf_op jit(solution)/shard_map/ppermute | solution.py:22
  72.0 6.5 %collective-permute-start.6 = (f32[1,64,256]{1,2,0:T(8,128)S(1)}, f32[1,64,256]{1,2,0:T(8,128)S(1)}, u32[]{:S(2)}, u32[]{:S(2)}) collective-permute-start(f32[1,64,256]{1,2,0:T(8,128)S(1)} %get-tuple-element.62), channel_id=1, source_target_pairs={{0,1},{1,2},{2,3},{3,4},{4,5},{5,6},{6,7},{8,9},{9,10},{10,11},{11... | collective-permute-start | bytes 196616 | tf_op jit(solution)/shard_map/ppermute | solution.py:19
  77.2 3.2 %collective-permute-start.7 = (f32[1,64,256]{1,2,0:T(8,128)S(1)}, f32[1,64,256]{1,2,0:T(8,128)S(1)}, u32[]{:S(2)}, u32[]{:S(2)}) collective-permute-start(f32[1,64,256]{1,2,0:T(8,128)S(1)} %get-tuple-element.63), channel_id=1, source_target_pairs={{1,0},{2,1},{3,2},{4,3},{5,4},{6,5},{7,6},{9,8},{10,9},{11,10},{12... | collective-permute-start | bytes 196616 | tf_op jit(solution)/shard_map/ppermute | solution.py:22
  95.9 12.5 %collective-permute-start.8 = (f32[1,64,256]{1,2,0:T(8,128)S(1)}, f32[1,64,256]{1,2,0:T(8,128)S(1)}, u32[]{:S(2)}, u32[]{:S(2)}) collective-permute-start(f32[1,64,256]{1,2,0:T(8,128)S(1)} %get-tuple-element.53), channel_id=1, source_target_pairs={{0,8},{8,16},{16,24},{1,9},{9,17},{17,25},{2,10},{10,18},{18,26},{... | collective-permute-start | bytes 196616 | tf_op jit(solution)/shard_map/ppermute | solution.py:19
  100.1 8.3 %collective-permute-start.9 = (f32[1,64,256]{1,2,0:T(8,128)S(1)}, f32[1,64,256]{1,2,0:T(8,128)S(1)}, u32[]{:S(2)}, u32[]{:S(2)}) collective-permute-start(f32[1,64,256]{1,2,0:T(8,128)S(1)} %get-tuple-element.56), channel_id=1, source_target_pairs={{8,0},{16,8},{24,16},{9,1},{17,9},{25,17},{10,2},{18,10},{26,18},{... | collective-permute-start | bytes 196616 | tf_op jit(solution)/shard_map/ppermute | solution.py:22
  101.4 7.0 %collective-permute-start.10 = (f32[1,64,256]{1,2,0:T(8,128)S(1)}, f32[1,64,256]{1,2,0:T(8,128)S(1)}, u32[]{:S(2)}, u32[]{:S(2)}) collective-permute-start(f32[1,64,256]{1,2,0:T(8,128)S(1)} %get-tuple-element.54), channel_id=1, source_target_pairs={{0,1},{1,2},{2,3},{3,4},{4,5},{5,6},{6,7},{8,9},{9,10},{10,11},{11... | collective-permute-start | bytes 196616 | tf_op jit(solution)/shard_map/ppermute | solution.py:19
  106.9 3.2 %collective-permute-start.11 = (f32[1,64,256]{1,2,0:T(8,128)S(1)}, f32[1,64,256]{1,2,0:T(8,128)S(1)}, u32[]{:S(2)}, u32[]{:S(2)}) collective-permute-start(f32[1,64,256]{1,2,0:T(8,128)S(1)} %get-tuple-element.55), channel_id=1, source_target_pairs={{1,0},{2,1},{3,2},{4,3},{5,4},{6,5},{7,6},{9,8},{10,9},{11,10},{12... | collective-permute-start | bytes 196616 | tf_op jit(solution)/shard_map/ppermute | solution.py:22
  125.9 58.7 %collective-permute-start.12 = (f32[1,64,256]{1,2,0:T(8,128)S(1)}, f32[1,64,256]{1,2,0:T(8,128)S(1)}, u32[]{:S(2)}, u32[]{:S(2)}) collective-permute-start(f32[1,64,256]{1,2,0:T(8,128)S(1)} %get-tuple-element.45), channel_id=1, source_target_pairs={{0,8},{8,16},{16,24},{1,9},{9,17},{17,25},{2,10},{10,18},{18,26},{... | collective-permute-start | bytes 196616 | tf_op jit(solution)/shard_map/ppermute | solution.py:19
  130.2 54.4 %collective-permute-start.13 = (f32[1,64,256]{1,2,0:T(8,128)S(1)}, f32[1,64,256]{1,2,0:T(8,128)S(1)}, u32[]{:S(2)}, u32[]{:S(2)}) collective-permute-start(f32[1,64,256]{1,2,0:T(8,128)S(1)} %get-tuple-element.48), channel_id=1, source_target_pairs={{8,0},{16,8},{24,16},{9,1},{17,9},{25,17},{10,2},{18,10},{26,18},{... | collective-permute-start | bytes 196616 | tf_op jit(solution)/shard_map/ppermute | solution.py:22
  131.5 53.1 %collective-permute-start.14 = (f32[1,64,256]{1,2,0:T(8,128)S(1)}, f32[1,64,256]{1,2,0:T(8,128)S(1)}, u32[]{:S(2)}, u32[]{:S(2)}) collective-permute-start(f32[1,64,256]{1,2,0:T(8,128)S(1)} %get-tuple-element.46), channel_id=1, source_target_pairs={{0,1},{1,2},{2,3},{3,4},{4,5},{5,6},{6,7},{8,9},{9,10},{10,11},{11... | collective-permute-start | bytes 196616 | tf_op jit(solution)/shard_map/ppermute | solution.py:19
  137.5 47.1 %collective-permute-start.15 = (f32[1,64,256]{1,2,0:T(8,128)S(1)}, f32[1,64,256]{1,2,0:T(8,128)S(1)}, u32[]{:S(2)}, u32[]{:S(2)}) collective-permute-start(f32[1,64,256]{1,2,0:T(8,128)S(1)} %get-tuple-element.47), channel_id=1, source_target_pairs={{1,0},{2,1},{3,2},{4,3},{5,4},{6,5},{7,6},{9,8},{10,9},{11,10},{12... | collective-permute-start | bytes 196616 | tf_op jit(solution)/shard_map/ppermute | solution.py:22
Sparse Core Ops, SparseCore 0:
  10.9 2.5 sort.21.cloned.1.call-done
  (1 shorter events, 0.0 us)
where the time goes:
time: 200 us
  local copies, waits for them, and re-layouts  55.2 us (28%)
  starting transfers between devices  50 us (25%)
  blocking collectives  43.5 us (22%)
  matrix products  20.1 us (10%)
  between operations  14.7 us (7%)
  waiting for transfers between devices  9.84 us (5%)
  other arithmetic  4.91 us (2%)
    psum x1, blocking collectives, local(): summed_terms = lax.psum(own_terms, ('space', 'bal'))  43.5 us
    ppermute x8, starting transfers between devices, padded(): lax.ppermute(lax.slice_in_dim(block, block.shape[dim] - width, None, axis...  39.5 us
    gather x8, local copies, waits for them, and re-layouts, local_order(): face_rows = jnp.take_along_axis(summed, inverse[:, None, :], axis=2)  28 us
    dot_general x3, matrix products, local(): product = jnp.dot(direction, gram_matrix, precision=lax.Precision.HIGHEST)  14.6 us
    gather x4, local copies, waits for them, and re-layouts, canon_order(): picked = jnp.take(field, position, axis=1)  11.2 us
    ppermute x8, starting transfers between devices, padded(): lax.ppermute(lax.slice_in_dim(block, 0, width, axis=dim), axis, backward)  10.5 us
    ppermute x8, waiting for transfers between devices, padded(): lax.ppermute(lax.slice_in_dim(block, 0, width, axis=dim), axis, backward)  9.81 us
    gather x2, local copies, waits for them, and re-layouts, local(): jnp.take_along_axis(live_canon, inverse, axis=1).reshape(1, columns)  9.15 us
  transfers between devices with their start and end apart: 16, of which 4 were waited for; matrix products, arithmetic and copies ran while one was open for 1% of the time, Pallas kernels for 0%

commit v1 on v0

v1 whole, which is shorter than its diff:
```python
import functools
import math

import jax
import jax.numpy as jnp
from jax import lax
from jax.experimental import pallas as pl
from jax.experimental.pallas import tpu as pltpu
from jax.sharding import PartitionSpec as P

BLOCK_ROWS = 512
ITERS = 3
FACES = 4
SEND_ORDER = (0, 1, 2, 3)
WAIT_ORDER = (2, 3, 0, 1)
MESH = pl.DeviceIdType.MESH
CONTRACT_LAST = (((1,), (1,)), ((), ()))
CONTRACT_MIDDLE = (((1,), (0,)), ((), ()))


def chebyshev_constants(iface, rows):
    upper = 2.6 * (1.0 + math.sqrt(iface / rows)) ** 2 + 4.0
    lower = 0.5
    center = (upper + lower) / 2.0
    half_span = (upper - lower) / 2.0
    return (center, half_span, center / half_span)


def parts(value, count):
    taken = []
    rest = value
    for index in range(count):
        part = rest.astype(jnp.bfloat16)
        taken.append(part)
        if index + 1 < count:
            rest = rest - part.astype(jnp.float32)
    return jnp.concatenate(taken, axis=0)


def product(value, matrix, dims, count=2):
    rows = value.shape[0]
    stacked = lax.dot_general(
        parts(value, count), matrix, dims, preferred_element_type=jnp.float32
    )
    total = stacked[:rows]
    for index in range(1, count):
        total = total + stacked[index * rows : (index + 1) * rows]
    return total


def kernel(
    n_space, n_bal,
    lengths_ref, enrich_ref, maps_ref, compliance_ref, contact_ref, loads_ref, panel_hbm,
    solution_ref, residual_ref, violation_ref,
    panel, kept, onehot, diag, direction, total, residual, send, recv, bal_sums, space_sums, own_bal, own_space,
    panel_sem, send_sem, recv_sem, bal_send, bal_recv, space_send, space_recv,
):
    me_s = lax.axis_index("space")
    me_b = lax.axis_index("bal")
    rows, columns = panel.shape
    face_len = columns // FACES
    loads = loads_ref.shape[0]
    center, half_span, ratio_c = chebyshev_constants(columns, rows)

    panel_copy = pltpu.make_async_copy(panel_hbm, panel, panel_sem)
    panel_copy.start()

    barrier = pltpu.get_barrier_semaphore()
    for step in range(1, n_bal):
        pl.semaphore_signal(
            barrier, inc=1, device_id={"bal": lax.rem(me_b + step, n_bal)}, device_id_type=MESH
        )
    for step in range(1, n_space):
        pl.semaphore_signal(
            barrier, inc=1, device_id={"space": lax.rem(me_s + step, n_space)}, device_id_type=MESH
        )

    present = (me_s > 0, me_s < n_space - 1, me_b > 0, me_b < n_bal - 1)
    across = (
        {"space": jnp.maximum(me_s - 1, 0)},
        {"space": jnp.minimum(me_s + 1, n_space - 1)},
        {"bal": jnp.maximum(me_b - 1, 0)},
        {"bal": jnp.minimum(me_b + 1, n_bal - 1)},
    )

    def face_copy(turn, face):
        return pltpu.make_async_remote_copy(
            src_ref=send.at[turn, face],
            dst_ref=recv.at[turn, face ^ 1],
            send_sem=send_sem.at[turn, face],
            recv_sem=recv_sem.at[turn, face ^ 1],
            device_id=across[face],
            device_id_type=MESH,
        )

    def start_face(turn, face):
        @pl.when(present[face])
        def _():
            face_copy(turn, face).start()

    def wait_face(turn, face):
        @pl.when(present[face])
        def _():
            face_copy(turn, face ^ 1).wait_recv()

    def span(face):
        return slice(face * face_len, (face + 1) * face_len)

    row_of = lax.broadcasted_iota(jnp.int32, (face_len, face_len), 0)
    slot_of = lax.broadcasted_iota(jnp.int32, (face_len, face_len), 1)
    for face in range(FACES):
        table = jnp.broadcast_to(maps_ref[face : face + 1, :], (face_len, face_len))
        hit = (row_of == table) & (slot_of < lengths_ref[0, face])
        onehot[face] = jnp.where(hit, 1.0, 0.0).astype(jnp.bfloat16)

    for face in SEND_ORDER:
        send[0, face] = product(loads_ref[:, span(face)], onehot[face], CONTRACT_MIDDLE)

    pl.semaphore_wait(barrier, n_bal - 1 + n_space - 1)
    for face in SEND_ORDER:
        start_face(0, face)

    for face in range(FACES):
        @pl.when(jnp.logical_not(present[face]))
        def _():
            for turn in range(ITERS + 1):
                recv[turn, face] = jnp.zeros((loads, face_len), jnp.float32)

    for face in range(FACES):
        wide = jnp.broadcast_to(compliance_ref[:, span(face)], (16, face_len))
        diag[:, span(face)] = product(wide, onehot[face], CONTRACT_MIDDLE, 3)

    lane = 128
    contact = contact_ref[...]
    groups = columns // lane
    group_rows = max(groups, 8)
    group_of = lax.broadcasted_iota(jnp.int32, (group_rows, contact.shape[1]), 0)
    place_of = lax.broadcasted_iota(jnp.int32, (lane, contact.shape[1]), 0)
    in_group = jnp.where(group_of == lax.shift_right_logical(contact, 7), 1.0, 0.0)
    at_place = jnp.where(place_of == (contact & (lane - 1)), 1.0, 0.0)
    counts = lax.dot_general(
        in_group.astype(jnp.bfloat16), at_place.astype(jnp.bfloat16), CONTRACT_LAST,
        preferred_element_type=jnp.float32,
    )

    panel_copy.wait()
    live_rows = enrich_ref[0, 0] * BLOCK_ROWS
    keep = lax.broadcasted_iota(jnp.int32, (rows, face_len), 0) < live_rows
    for face in range(FACES):
        picked = jnp.dot(panel[:, span(face)], onehot[face], preferred_element_type=jnp.float32)
        kept[:, span(face)] = jnp.where(keep, picked, 0.0).astype(jnp.bfloat16)

    def project(face, running):
        term = lax.dot_general(
            parts(direction[:, span(face)], 2), kept[:, span(face)], CONTRACT_LAST,
            preferred_element_type=jnp.float32,
        )
        return term if running is None else running + term

    running = None
    for face in WAIT_ORDER:
        wait_face(0, face)
        first = send[0, face] + recv[0, face]
        residual[:, span(face)] = first
        direction[:, span(face)] = first / center
        total[:, span(face)] = first / center
        running = project(face, running)

    cheb_rho = 1.0 / ratio_c
    for iteration in range(ITERS):
        turn = iteration + 1
        last = turn == ITERS
        if last:
            weighted = jnp.zeros((loads, lane), jnp.float32)
            for face in range(FACES):
                local = product(total[:, span(face)], onehot[face], CONTRACT_LAST)
                solution_ref[:, span(face)] = local
                negative = jnp.minimum(local, 0.0)
                squares = negative * negative
                for piece in range(face_len // lane):
                    group = face * (face_len // lane) + piece
                    weighted = weighted + squares[:, piece * lane : (piece + 1) * lane] * counts[group : group + 1, :]
            pieces = parts(weighted, 3)
            ones = jnp.ones((16, lane), jnp.bfloat16)
            spread = lax.dot_general(ones, pieces, CONTRACT_LAST, preferred_element_type=jnp.float32)
            terms = spread[:8, :loads] + spread[:8, loads : 2 * loads] + spread[:8, 2 * loads :]
            own_bal[:, :loads] = terms
            own_bal[:, loads:] = jnp.zeros((8, own_bal.shape[1] - loads), jnp.float32)
            bal_sums[me_b] = own_bal[...]
            for step in range(1, n_bal):
                pltpu.make_async_remote_copy(
                    src_ref=own_bal, dst_ref=bal_sums.at[me_b],
                    send_sem=bal_send.at[step], recv_sem=bal_recv.at[step],
                    device_id={"bal": lax.rem(me_b + step, n_bal)}, device_id_type=MESH,
                ).start()

        projected = parts(running[:loads] + running[loads:], 2)
        for face in SEND_ORDER:
            stacked = jnp.dot(projected, kept[:, span(face)], preferred_element_type=jnp.float32)
            send[turn, face] = (
                stacked[:loads] + stacked[loads:] + direction[:, span(face)] * diag[0:1, span(face)]
            )
            start_face(turn, face)

        if last:
            for step in range(1, n_bal):
                source = lax.rem(me_b + n_bal - step, n_bal)
                pltpu.make_async_remote_copy(
                    src_ref=own_bal, dst_ref=bal_sums.at[source],
                    send_sem=bal_send.at[step], recv_sem=bal_recv.at[step],
                    device_id={"bal": source}, device_id_type=MESH,
                ).wait()
            summed = bal_sums[0]
            for index in range(1, n_bal):
                summed = summed + bal_sums[index]
            own_space[...] = summed
            space_sums[me_s] = summed
            for step in range(1, n_space):
                pltpu.make_async_remote_copy(
                    src_ref=own_space, dst_ref=space_sums.at[me_s],
                    send_sem=space_send.at[step], recv_sem=space_recv.at[step],
                    device_id={"space": lax.rem(me_s + step, n_space)}, device_id_type=MESH,
                ).start()
            for face in WAIT_ORDER:
                wait_face(turn, face)
                final = residual[:, span(face)] - (send[turn, face] + recv[turn, face])
                residual_ref[:, span(face)] = product(final, onehot[face], CONTRACT_LAST)
        else:
            rho_next = 1.0 / (2.0 * ratio_c - cheb_rho)
            running = None
            for face in WAIT_ORDER:
                wait_face(turn, face)
                updated = residual[:, span(face)] - (send[turn, face] + recv[turn, face])
                residual[:, span(face)] = updated
                moved = rho_next * cheb_rho * direction[:, span(face)] + 2.0 * rho_next / half_span * updated
                direction[:, span(face)] = moved
                total[:, span(face)] = total[:, span(face)] + moved
                running = project(face, running)
            cheb_rho = rho_next

    for step in range(1, n_space):
        source = lax.rem(me_s + n_space - step, n_space)
        pltpu.make_async_remote_copy(
            src_ref=own_space, dst_ref=space_sums.at[source],
            send_sem=space_send.at[step], recv_sem=space_recv.at[step],
            device_id={"space": source}, device_id_type=MESH,
        ).wait()
    summed = space_sums[0]
    for index in range(1, n_space):
        summed = summed + space_sums[index]
    violation_ref[...] = jnp.sqrt(summed[0:1, :loads] + 1e-06)

    for turn in range(ITERS + 1):
        for face in range(FACES):
            @pl.when(present[face])
            def _():
                face_copy(turn, face).wait_send()


def local(n_space, n_bal, panels, enrich, compliance, loads, face_maps, face_lengths, contact):
    rows, columns = panels.shape[2:]
    n_loads = loads.shape[2]
    face_len = columns // FACES
    width = -(-n_loads // 128) * 128
    vmem = pl.BlockSpec(memory_space=pltpu.VMEM)
    smem = pl.BlockSpec(memory_space=pltpu.SMEM)
    turns = ITERS + 1
    flops = 2 * rows * columns * (face_len + ITERS * 4 * n_loads)
    field = (n_loads, columns)
    out = pl.pallas_call(
        functools.partial(kernel, n_space, n_bal),
        out_shape=(
            jax.ShapeDtypeStruct(field, jnp.float32),
            jax.ShapeDtypeStruct(field, jnp.float32),
            jax.ShapeDtypeStruct((1, n_loads), jnp.float32),
        ),
        in_specs=[smem, smem, vmem, vmem, vmem, vmem, pl.BlockSpec(memory_space=pl.ANY)],
        out_specs=(vmem, vmem, vmem),
        scratch_shapes=[
            pltpu.VMEM((rows, columns), jnp.bfloat16),
            pltpu.VMEM((rows, columns), jnp.bfloat16),
            pltpu.VMEM((FACES, face_len, face_len), jnp.bfloat16),
            pltpu.VMEM((16, columns), jnp.float32),
            pltpu.VMEM(field, jnp.float32),
            pltpu.VMEM(field, jnp.float32),
            pltpu.VMEM(field, jnp.float32),
            pltpu.VMEM((turns, FACES, n_loads, face_len), jnp.float32),
            pltpu.VMEM((turns, FACES, n_loads, face_len), jnp.float32),
            pltpu.VMEM((n_bal, 8, width), jnp.float32),
            pltpu.VMEM((n_space, 8, width), jnp.float32),
            pltpu.VMEM((8, width), jnp.float32),
            pltpu.VMEM((8, width), jnp.float32),
            pltpu.SemaphoreType.DMA,
            pltpu.SemaphoreType.DMA((turns, FACES)),
            pltpu.SemaphoreType.DMA((turns, FACES)),
            pltpu.SemaphoreType.DMA((n_bal,)),
            pltpu.SemaphoreType.DMA((n_bal,)),
            pltpu.SemaphoreType.DMA((n_space,)),
            pltpu.SemaphoreType.DMA((n_space,)),
        ],
        compiler_params=pltpu.CompilerParams(
            collective_id=0, has_side_effects=True, vmem_limit_bytes=48 * 1024 * 1024
        ),
        cost_estimate=pl.CostEstimate(
            flops=flops, bytes_accessed=2 * rows * columns + 12 * n_loads * columns, transcendentals=n_loads
        ),
        name="feti",
    )(
        face_lengths[0], enrich, face_maps[0, 0], compliance[0], contact[0], loads[0, 0], panels[0, 0]
    )
    return (out[0][None, None], out[1][None, None], out[2][0])


def solution(mesh):
    in_specs = (
        P("space", "bal", None, None),
        P("space", "bal"),
        P("space", "bal", None),
        P("space", "bal", None, None),
        P("space", "bal", None, None),
        P("space", "bal", None),
        P("space", "bal", None),
    )
    out_specs = (P("space", "bal", None, None), P("space", "bal", None, None), P())
    body = functools.partial(local, mesh.shape["space"], mesh.shape["bal"])
    return jax.shard_map(body, mesh=mesh, in_specs=in_specs, out_specs=out_specs, check_vma=False)
```

time: 200 us -> 36.6 us (0.18)
  starting transfers between devices: 50 us -> 0 us
  local copies, waits for them, and re-layouts: 55.2 us -> 7.13 us
  blocking collectives: 43.5 us -> 0 us
  Pallas kernels: 0 us -> 27.9 us
  matrix products: 20.1 us -> 0 us
  between operations: 14.7 us -> 1.3 us
  waiting for transfers between devices: 9.84 us -> 0 us
  other arithmetic: 4.91 us -> 0 us
    ppermute x16 -> x0, starting transfers between devices: 50 us -> none  [the longest x8 39.5 us: padded(): lax.ppermute(lax.slice_in_dim(block, block.shape[dim] - width, None, axis...]
    gather x15 -> x0, local copies, waits for them, and re-layouts: 49 us -> none  [the longest x8 28 us: local_order(): face_rows = jnp.take_along_axis(summed, inverse[:, None, :], axis=2)]
    psum x1 -> x0, blocking collectives: 43.5 us -> none  [local(): summed_terms = lax.psum(own_terms, ('space', 'bal'))]
    pallas_call x0 -> x1, Pallas kernels: none -> 27.9 us  [local(): pl.pallas_call(functools.partial(kernel, n_space, n_bal), out_shape=(jax....]
    dot_general x4 -> x0, matrix products: 20.1 us -> none  [the longest x3 14.6 us: local(): product = jnp.dot(direction, gram_matrix, precision=lax.Precision.HIGHEST)]
    ppermute x16 -> x0, waiting for transfers between devices: 9.84 us -> none  [the longest x8 9.81 us: padded(): lax.ppermute(lax.slice_in_dim(block, 0, width, axis=dim), axis, backward)]
    unnamed x20 -> x15, local copies, waits for them, and re-layouts: 0.27 us -> 7.13 us
    broadcast_in_dim x1 -> x0, local copies, waits for them, and re-layouts: 2.48 us -> none  [local(): jnp.zeros((columns, columns), jnp.float32)]
  transfers between devices with their start and end apart: 16 -> 0, of which waited for: 4 -> 0; matrix products, arithmetic and copies ran while one was open for 1% -> 0% of each run, Pallas kernels for 0% -> 0%
where the time goes in v1:
time: 36.6 us; the launch traced here: 36.3 us
  Pallas kernels  27.9 us (76%)
  local copies, waits for them, and re-layouts  7.13 us (19%)
  between operations  1.3 us (4%)
    pallas_call x1, Pallas kernels, local(): pl.pallas_call(functools.partial(kernel, n_space, n_bal), out_shape=(jax....  27.9 us
    unnamed x15, local copies, waits for them, and re-layouts  7.13 us

profile of v1, /device:TPU:0, one launch (start us, length us, event | category | flops | bytes accessed | tf_op | source)
XLA Modules:
  0.0 36.3 jit_solution(9442299201159931953)
XLA Ops:
  1.3 0.0 copy-start
  1.3 1.6 %copy-done = bf16[1,1,1024,1024]{3,2,1,0:T(8,128)(2,1)S(1)} copy-done((bf16[1,1,1024,1024]{3,2,1,0:T(8,128)(2,1)S(1)}, bf16[1,1,1024,1024]{3,2,1,0:T(8,128)(2,1)}, u32[]{:S(2)}) %copy-start) | copy-done | bytes 2097176
  2.9 0.0 copy-start.1
  2.9 0.9 %copy-done.1 = f32[1,1,64,1024]{3,2,1,0:T(8,128)S(1)} copy-done((f32[1,1,64,1024]{3,2,1,0:T(8,128)S(1)}, f32[1,1,64,1024]{3,2,1,0:T(8,128)}, u32[]{:S(2)}) %copy-start.1) | copy-done | bytes 262168
  3.8 0.0 copy-start.2
  3.8 0.7 %copy-done.2 = s32[1,1,4,256]{3,2,1,0:T(4,128)S(1)} copy-done((s32[1,1,4,256]{3,2,1,0:T(4,128)S(1)}, s32[1,1,4,256]{3,2,1,0:T(4,128)}, u32[]{:S(2)}) %copy-start.2) | copy-done | bytes 4120
  4.5 0.0 copy-start.3
  4.5 0.7 %copy-done.3 = f32[1,1,1024]{2,1,0:T(1,128)S(1)} copy-done((f32[1,1,1024]{2,1,0:T(1,128)S(1)}, f32[1,1,1024]{2,1,0:T(1,128)}, u32[]{:S(2)}) %copy-start.3) | copy-done | bytes 4120
  5.2 0.0 copy-start.4
  5.2 0.7 %copy-done.4 = s32[1,1,4]{2,1,0:T(1,128)S(1)} copy-done((s32[1,1,4]{2,1,0:T(1,128)S(1)}, s32[1,1,4]{2,1,0:T(1,128)}, u32[]{:S(2)}) %copy-start.4) | copy-done | bytes 40
  5.9 0.0 copy-start.5
  5.9 0.7 %copy-done.5 = s32[1,1,128]{2,1,0:T(1,128)S(1)} copy-done((s32[1,1,128]{2,1,0:T(1,128)S(1)}, s32[1,1,128]{2,1,0:T(1,128)}, u32[]{:S(2)}) %copy-start.5) | copy-done | bytes 536
  6.5 27.9 %feti.1 = (f32[64,1024]{1,0:T(8,128)S(1)}, f32[64,1024]{1,0:T(8,128)S(1)}, f32[1,64]{1,0:T(1,128)S(1)}) custom-call(s32[1,4]{1,0:T(1,128)S(1)} %bitcast.15, s32[1,1]{1,0:T(1,128)S(6)} %copy.13.enrich_ref, s32[4,256]{1,0:T(4,128)S(1)} %bitcast.13, f32[1,1024]{1,0:T(1,128)S(1)} %bitcast.14, s32[1,128]{1,0:T(1,128)S(1)} %bitcast.16, f32[64,1024]{1,0:T(8,128)S(1)} %bitcast.12, ...), custom_call_target="tpu_custom_call" | custom-call | flops 2147483648 | bytes 2883584 | tf_op jit(solution)/shard_map/feti/pallas_call | solution.py:270
  34.4 0.7 %copy.14 = f32[1,1,64,1024]{3,2,1,0:T(8,128)} copy(f32[1,1,64,1024]{3,2,1,0:T(8,128)S(1)} %bitcast.10) | data formatting | bytes 524288
  35.1 0.7 %copy.15 = f32[1,1,64,1024]{3,2,1,0:T(8,128)} copy(f32[1,1,64,1024]{3,2,1,0:T(8,128)S(1)} %bitcast.9) | data formatting | bytes 524288
  35.8 0.5 %copy.16 = f32[64]{0:T(128)} copy(f32[64]{0:T(128)S(1)} %bitcast.17) | data formatting | bytes 512
Async XLA Ops:
  1.3 1.6 %copy-start = (bf16[1,1,1024,1024]{3,2,1,0:T(8,128)(2,1)S(1)}, bf16[1,1,1024,1024]{3,2,1,0:T(8,128)(2,1)}, u32[]{:S(2)}) copy-start(bf16[1,1,1024,1024]{3,2,1,0:T(8,128)(2,1)} %param.7) | copy-start | bytes 6291460
  2.9 0.9 %copy-start.1 = (f32[1,1,64,1024]{3,2,1,0:T(8,128)S(1)}, f32[1,1,64,1024]{3,2,1,0:T(8,128)}, u32[]{:S(2)}) copy-start(f32[1,1,64,1024]{3,2,1,0:T(8,128)} %param.10) | copy-start | bytes 786436
  3.8 0.7 %copy-start.2 = (s32[1,1,4,256]{3,2,1,0:T(4,128)S(1)}, s32[1,1,4,256]{3,2,1,0:T(4,128)}, u32[]{:S(2)}) copy-start(s32[1,1,4,256]{3,2,1,0:T(4,128)} %param.11) | copy-start | bytes 12292
  4.5 0.7 %copy-start.3 = (f32[1,1,1024]{2,1,0:T(1,128)S(1)}, f32[1,1,1024]{2,1,0:T(1,128)}, u32[]{:S(2)}) copy-start(f32[1,1,1024]{2,1,0:T(1,128)} %param.9) | copy-start | bytes 12292
  5.2 0.7 %copy-start.4 = (s32[1,1,4]{2,1,0:T(1,128)S(1)}, s32[1,1,4]{2,1,0:T(1,128)}, u32[]{:S(2)}) copy-start(s32[1,1,4]{2,1,0:T(1,128)} %param.12) | copy-start | bytes 52
  5.9 0.7 %copy-start.5 = (s32[1,1,128]{2,1,0:T(1,128)S(1)}, s32[1,1,128]{2,1,0:T(1,128)}, u32[]{:S(2)}) copy-start(s32[1,1,128]{2,1,0:T(1,128)} %param.13) | copy-start | bytes 1540

commit v2 on v1

--- a/solution.py
+++ b/solution.py
@@ -11,6 +11,7 @@
 BLOCK_ROWS = 512
 ITERS = 3
 FACES = 4
+VMEM_BYTES = 64 * 1024 * 1024
 SEND_ORDER = (0, 1, 2, 3)
 WAIT_ORDER = (2, 3, 0, 1)
 MESH = pl.DeviceIdType.MESH
@@ -50,10 +51,11 @@
 
 def kernel(
     n_space, n_bal,
-    lengths_ref, enrich_ref, maps_ref, compliance_ref, contact_ref, loads_ref, panel_hbm,
-    solution_ref, residual_ref, violation_ref,
-    panel, kept, onehot, diag, direction, total, residual, send, recv, bal_sums, space_sums, own_bal, own_space,
-    panel_sem, send_sem, recv_sem, bal_send, bal_recv, space_send, space_recv,
+    lengths_hbm, enrich_ref, maps_hbm, compliance_hbm, contact_hbm, loads_hbm, panel_hbm,
+    solution_hbm, residual_hbm, violation_hbm,
+    lengths_ref, maps_ref, compliance_ref, contact_ref, loads_ref,
+    solution_ref, residual_ref, violation_ref, turned, panel, kept, kept_turned, onehot, diag, direction, total, residual, send, recv, bal_sums, space_sums, own_bal, own_space,
+    input_sem, output_sem, send_sem, recv_sem, bal_send, bal_recv, space_send, space_recv,
 ):
     me_s = lax.axis_index("space")
     me_b = lax.axis_index("bal")
@@ -62,8 +64,16 @@
     loads = loads_ref.shape[0]
     center, half_span, ratio_c = chebyshev_constants(columns, rows)
 
-    panel_copy = pltpu.make_async_copy(panel_hbm, panel, panel_sem)
-    panel_copy.start()
+    inputs = (
+        (maps_hbm, maps_ref), (lengths_hbm, lengths_ref), (loads_hbm, loads_ref), (panel_hbm, panel),
+        (compliance_hbm, compliance_ref), (contact_hbm, contact_ref),
+    )
+    copies = [
+        pltpu.make_async_copy(source, target, input_sem.at[index])
+        for index, (source, target) in enumerate(inputs)
+    ]
+    for copy in copies:
+        copy.start()
 
     barrier = pltpu.get_barrier_semaphore()
     for step in range(1, n_bal):
@@ -106,6 +116,8 @@
     def span(face):
         return slice(face * face_len, (face + 1) * face_len)
 
+    copies[0].wait()
+    copies[1].wait()
     row_of = lax.broadcasted_iota(jnp.int32, (face_len, face_len), 0)
     slot_of = lax.broadcasted_iota(jnp.int32, (face_len, face_len), 1)
     for face in range(FACES):
@@ -113,6 +125,7 @@
         hit = (row_of == table) & (slot_of < lengths_ref[0, face])
         onehot[face] = jnp.where(hit, 1.0, 0.0).astype(jnp.bfloat16)
 
+    copies[2].wait()
     for face in SEND_ORDER:
         send[0, face] = product(loads_ref[:, span(face)], onehot[face], CONTRACT_MIDDLE)
 
@@ -126,7 +139,10 @@
             for turn in range(ITERS + 1):
                 recv[turn, face] = jnp.zeros((loads, face_len), jnp.float32)
 
+    for index in range(4, len(copies)):
+        copies[index].wait()
     for face in range(FACES):
+        turned[face] = onehot[face].T
         wide = jnp.broadcast_to(compliance_ref[:, span(face)], (16, face_len))
         diag[:, span(face)] = product(wide, onehot[face], CONTRACT_MIDDLE, 3)
 
@@ -143,17 +159,18 @@
         preferred_element_type=jnp.float32,
     )
 
-    panel_copy.wait()
+    copies[3].wait()
     live_rows = enrich_ref[0, 0] * BLOCK_ROWS
     keep = lax.broadcasted_iota(jnp.int32, (rows, face_len), 0) < live_rows
     for face in range(FACES):
         picked = jnp.dot(panel[:, span(face)], onehot[face], preferred_element_type=jnp.float32)
-        kept[:, span(face)] = jnp.where(keep, picked, 0.0).astype(jnp.bfloat16)
+        masked = jnp.where(keep, picked, 0.0).astype(jnp.bfloat16)
+        kept[:, span(face)] = masked
+        kept_turned[span(face), :] = masked.T
 
     def project(face, running):
-        term = lax.dot_general(
-            parts(direction[:, span(face)], 2), kept[:, span(face)], CONTRACT_LAST,
-            preferred_element_type=jnp.float32,
+        term = jnp.dot(
+            parts(direction[:, span(face)], 2), kept_turned[span(face), :], preferred_element_type=jnp.float32
         )
         return term if running is None else running + term
 
@@ -173,7 +190,7 @@
         if last:
             weighted = jnp.zeros((loads, lane), jnp.float32)
             for face in range(FACES):
-                local = product(total[:, span(face)], onehot[face], CONTRACT_LAST)
+                local = product(total[:, span(face)], turned[face], CONTRACT_MIDDLE)
                 solution_ref[:, span(face)] = local
                 negative = jnp.minimum(local, 0.0)
                 squares = negative * negative
@@ -221,10 +238,12 @@
                     send_sem=space_send.at[step], recv_sem=space_recv.at[step],
                     device_id={"space": lax.rem(me_s + step, n_space)}, device_id_type=MESH,
                 ).start()
+            solution_copy = pltpu.make_async_copy(solution_ref, solution_hbm, output_sem.at[0])
+            solution_copy.start()
             for face in WAIT_ORDER:
                 wait_face(turn, face)
                 final = residual[:, span(face)] - (send[turn, face] + recv[turn, face])
-                residual_ref[:, span(face)] = product(final, onehot[face], CONTRACT_LAST)
+                residual_ref[:, span(face)] = product(final, turned[face], CONTRACT_MIDDLE)
         else:
             rho_next = 1.0 / (2.0 * ratio_c - cheb_rho)
             running = None
@@ -238,6 +257,8 @@
                 running = project(face, running)
             cheb_rho = rho_next
 
+    residual_copy = pltpu.make_async_copy(residual_ref, residual_hbm, output_sem.at[1])
+    residual_copy.start()
     for step in range(1, n_space):
         source = lax.rem(me_s + n_space - step, n_space)
         pltpu.make_async_remote_copy(
@@ -249,12 +270,28 @@
     for index in range(1, n_space):
         summed = summed + space_sums[index]
     violation_ref[...] = jnp.sqrt(summed[0:1, :loads] + 1e-06)
+    violation_copy = pltpu.make_async_copy(violation_ref, violation_hbm, output_sem.at[2])
+    violation_copy.start()
 
     for turn in range(ITERS + 1):
         for face in range(FACES):
             @pl.when(present[face])
             def _():
                 face_copy(turn, face).wait_send()
+    solution_copy.wait()
+    residual_copy.wait()
+    violation_copy.wait()
+
+
+def finish(solution_in, residual_in, violation_in, solution_out, residual_out, violation_out, sems):
+    pairs = ((solution_in, solution_out), (residual_in, residual_out), (violation_in, violation_out))
+    copies = [
+        pltpu.make_async_copy(source, target, sems.at[index]) for index, (source, target) in enumerate(pairs)
+    ]
+    for copy in copies:
+        copy.start()
+    for copy in copies:
+        copy.wait()
 
 
 def local(n_space, n_bal, panels, enrich, compliance, loads, face_maps, face_lengths, contact):
@@ -262,8 +299,7 @@
     n_loads = loads.shape[2]
     face_len = columns // FACES
     width = -(-n_loads // 128) * 128
-    vmem = pl.BlockSpec(memory_space=pltpu.VMEM)
-    smem = pl.BlockSpec(memory_space=pltpu.SMEM)
+    hbm = pl.BlockSpec(memory_space=pltpu.HBM)
     turns = ITERS + 1
     flops = 2 * rows * columns * (face_len + ITERS * 4 * n_loads)
     field = (n_loads, columns)
@@ -274,9 +310,19 @@
             jax.ShapeDtypeStruct(field, jnp.float32),
             jax.ShapeDtypeStruct((1, n_loads), jnp.float32),
         ),
-        in_specs=[smem, smem, vmem, vmem, vmem, vmem, pl.BlockSpec(memory_space=pl.ANY)],
-        out_specs=(vmem, vmem, vmem),
+        in_specs=[hbm, pl.BlockSpec(memory_space=pltpu.SMEM)] + [hbm] * 5,
+        out_specs=(hbm, hbm, hbm),
         scratch_shapes=[
+            pltpu.SMEM((1, FACES), jnp.int32),
+            pltpu.VMEM((FACES, face_len), jnp.int32),
+            pltpu.VMEM((1, columns), jnp.float32),
+            pltpu.VMEM((1, contact.shape[2]), jnp.int32),
+            pltpu.VMEM(field, jnp.float32),
+            pltpu.VMEM(field, jnp.float32),
+            pltpu.VMEM(field, jnp.float32),
+            pltpu.VMEM((1, n_loads), jnp.float32),
+            pltpu.VMEM((FACES, face_len, face_len), jnp.bfloat16),
+            pltpu.VMEM((rows, columns), jnp.bfloat16),
             pltpu.VMEM((rows, columns), jnp.bfloat16),
             pltpu.VMEM((rows, columns), jnp.bfloat16),
             pltpu.VMEM((FACES, face_len, face_len), jnp.bfloat16),
@@ -290,7 +336,8 @@
             pltpu.VMEM((n_space, 8, width), jnp.float32),
             pltpu.VMEM((8, width), jnp.float32),
             pltpu.VMEM((8, width), jnp.float32),
-            pltpu.SemaphoreType.DMA,
+            pltpu.SemaphoreType.DMA((6,)),
+            pltpu.SemaphoreType.DMA((3,)),
             pltpu.SemaphoreType.DMA((turns, FACES)),
             pltpu.SemaphoreType.DMA((turns, FACES)),
             pltpu.SemaphoreType.DMA((n_bal,)),
@@ -299,7 +346,7 @@
             pltpu.SemaphoreType.DMA((n_space,)),
         ],
         compiler_params=pltpu.CompilerParams(
-            collective_id=0, has_side_effects=True, vmem_limit_bytes=48 * 1024 * 1024
+            collective_id=0, has_side_effects=True, vmem_limit_bytes=VMEM_BYTES
         ),
         cost_estimate=pl.CostEstimate(
             flops=flops, bytes_accessed=2 * rows * columns + 12 * n_loads * columns, transcendentals=n_loads
@@ -308,7 +355,20 @@
     )(
         face_lengths[0], enrich, face_maps[0, 0], compliance[0], contact[0], loads[0, 0], panels[0, 0]
     )
-    return (out[0][None, None], out[1][None, None], out[2][0])
+    finished = pl.pallas_call(
+        finish,
+        out_shape=(
+            jax.ShapeDtypeStruct(field, jnp.float32),
+            jax.ShapeDtypeStruct(field, jnp.float32),
+            jax.ShapeDtypeStruct((1, n_loads), jnp.float32),
+        ),
+        in_specs=[hbm] * 3,
+        out_specs=(hbm, hbm, hbm),
+        scratch_shapes=[pltpu.SemaphoreType.DMA((3,))],
+        compiler_params=pltpu.CompilerParams(vmem_limit_bytes=VMEM_BYTES),
+        name="finish",
+    )(*out)
+    return (finished[0][None, None], finished[1][None, None], finished[2][0])
 
 
 def solution(mesh):

time: 36.6 us -> 45.3 us (1.24)
  Pallas kernels: 27.9 us -> 43.8 us
  local copies, waits for them, and re-layouts: 7.13 us -> 0 us
    pallas_call x0 -> x1, Pallas kernels: none -> 17 us  [local(): pl.pallas_call(finish, out_shape=(jax.ShapeDtypeStruct(field, jnp.float32...]
    unnamed x15 -> x0, local copies, waits for them, and re-layouts: 7.13 us -> none
    pallas_call x1, Pallas kernels: 27.9 us -> 26.8 us  [local(): pl.pallas_call(functools.partial(kernel, n_space, n_bal), out_shape=(jax....]
where the time goes in v2:
time: 45.3 us; the launch traced here: 45.1 us
  Pallas kernels  43.8 us (97%)
  between operations  1.29 us (3%)
    pallas_call x1, Pallas kernels, local(): pl.pallas_call(functools.partial(kernel, n_space, n_bal), out_shape=(jax....  26.8 us
    pallas_call x1, Pallas kernels, local(): pl.pallas_call(finish, out_shape=(jax.ShapeDtypeStruct(field, jnp.float32...  17 us

profile of v2, /device:TPU:0, one launch (start us, length us, event | category | flops | bytes accessed | tf_op | source)
XLA Modules:
  0.0 45.1 jit_solution(373956467391815750)
XLA Ops:
  1.3 26.8 %feti.1 = (f32[64,1024]{1,0:T(8,128)}, f32[64,1024]{1,0:T(8,128)}, f32[1,64]{1,0:T(1,128)}) custom-call(s32[1,4]{1,0:T(1,128)} %bitcast.15, s32[1,1]{1,0:T(1,128)S(6)} %copy.10.enrich_ref, s32[4,256]{1,0:T(4,128)} %bitcast.13, f32[1,1024]{1,0:T(1,128)} %bitcast.14, s32[1,128]{1,0:T(1,128)} %bitcast.16, f32[64,1024]{1,0:T(8,128)} %bitcast.10, ...), custom_call_target="tpu_custom_call" | custom-call | flops 2147483648 | bytes 2883584 | tf_op jit(solution)/shard_map/feti/pallas_call | solution.py:306
  28.1 17.0 %finish.1 = (f32[64,1024]{1,0:T(8,128)}, f32[64,1024]{1,0:T(8,128)}, f32[1,64]{1,0:T(1,128)}) custom-call(f32[64,1024]{1,0:T(8,128)} %get-tuple-element.9.solution_in, f32[64,1024]{1,0:T(8,128)} %get-tuple-element.10.residual_in, f32[1,64]{1,0:T(1,128)} %get-tuple-element.11.violation_in), custom_call_target="tpu_custom_call" | custom-call | tf_op jit(solution)/shard_map/finish/pallas_call | solution.py:358

commit v3 on v2

--- a/solution.py
+++ b/solution.py
@@ -11,6 +11,7 @@
 BLOCK_ROWS = 512
 ITERS = 3
 FACES = 4
+HALVES = 2
 VMEM_BYTES = 64 * 1024 * 1024
 SEND_ORDER = (0, 1, 2, 3)
 WAIT_ORDER = (2, 3, 0, 1)
@@ -54,7 +55,7 @@
     lengths_hbm, enrich_ref, maps_hbm, compliance_hbm, contact_hbm, loads_hbm, panel_hbm,
     solution_hbm, residual_hbm, violation_hbm,
     lengths_ref, maps_ref, compliance_ref, contact_ref, loads_ref,
-    solution_ref, residual_ref, violation_ref, turned, panel, kept, kept_turned, onehot, diag, direction, total, residual, send, recv, bal_sums, space_sums, own_bal, own_space,
+    solution_ref, residual_ref, violation_ref, turned, panel, kept, kept_turned, onehot, diag, direction, total, residual, violated, send, recv, bal_sums, space_sums, own_bal, own_space,
     input_sem, output_sem, send_sem, recv_sem, bal_send, bal_recv, space_send, space_recv,
 ):
     me_s = lax.axis_index("space")
@@ -92,26 +93,30 @@
         {"bal": jnp.maximum(me_b - 1, 0)},
         {"bal": jnp.minimum(me_b + 1, n_bal - 1)},
     )
-
-    def face_copy(turn, face):
+    part = loads // HALVES
+
+    def face_copy(turn, half, face):
         return pltpu.make_async_remote_copy(
-            src_ref=send.at[turn, face],
-            dst_ref=recv.at[turn, face ^ 1],
-            send_sem=send_sem.at[turn, face],
-            recv_sem=recv_sem.at[turn, face ^ 1],
+            src_ref=send.at[turn, half, face],
+            dst_ref=recv.at[turn, half, face ^ 1],
+            send_sem=send_sem.at[turn, half, face],
+            recv_sem=recv_sem.at[turn, half, face ^ 1],
             device_id=across[face],
             device_id_type=MESH,
         )
 
-    def start_face(turn, face):
+    def start_face(turn, half, face):
         @pl.when(present[face])
         def _():
-            face_copy(turn, face).start()
-
-    def wait_face(turn, face):
+            face_copy(turn, half, face).start()
+
+    def wait_face(turn, half, face):
         @pl.when(present[face])
         def _():
-            face_copy(turn, face ^ 1).wait_recv()
+            face_copy(turn, half, face ^ 1).wait_recv()
+
+    def lines(half):
+        return slice(half * part, (half + 1) * part)
 
     def span(face):
         return slice(face * face_len, (face + 1) * face_len)
@@ -127,17 +132,21 @@
 
     copies[2].wait()
     for face in SEND_ORDER:
-        send[0, face] = product(loads_ref[:, span(face)], onehot[face], CONTRACT_MIDDLE)
+        canonical = product(loads_ref[:, span(face)], onehot[face], CONTRACT_MIDDLE)
+        for half in range(HALVES):
+            send[0, half, face] = canonical[lines(half)]
 
     pl.semaphore_wait(barrier, n_bal - 1 + n_space - 1)
-    for face in SEND_ORDER:
-        start_face(0, face)
+    for half in range(HALVES):
+        for face in SEND_ORDER:
+            start_face(0, half, face)
 
     for face in range(FACES):
         @pl.when(jnp.logical_not(present[face]))
         def _():
             for turn in range(ITERS + 1):
-                recv[turn, face] = jnp.zeros((loads, face_len), jnp.float32)
+                for half in range(HALVES):
+                    recv[turn, half, face] = jnp.zeros((part, face_len), jnp.float32)
 
     for index in range(4, len(copies)):
         copies[index].wait()
@@ -168,97 +177,116 @@
         kept[:, span(face)] = masked
         kept_turned[span(face), :] = masked.T
 
-    def project(face, running):
+    def project(half, face, running):
         term = jnp.dot(
-            parts(direction[:, span(face)], 2), kept_turned[span(face), :], preferred_element_type=jnp.float32
+            parts(direction[lines(half), span(face)], 2), kept_turned[span(face), :],
+            preferred_element_type=jnp.float32,
         )
         return term if running is None else running + term
 
-    running = None
-    for face in WAIT_ORDER:
-        wait_face(0, face)
-        first = send[0, face] + recv[0, face]
-        residual[:, span(face)] = first
-        direction[:, span(face)] = first / center
-        total[:, span(face)] = first / center
-        running = project(face, running)
-
-    cheb_rho = 1.0 / ratio_c
-    for iteration in range(ITERS):
-        turn = iteration + 1
-        last = turn == ITERS
-        if last:
-            weighted = jnp.zeros((loads, lane), jnp.float32)
-            for face in range(FACES):
-                local = product(total[:, span(face)], turned[face], CONTRACT_MIDDLE)
-                solution_ref[:, span(face)] = local
-                negative = jnp.minimum(local, 0.0)
-                squares = negative * negative
-                for piece in range(face_len // lane):
-                    group = face * (face_len // lane) + piece
-                    weighted = weighted + squares[:, piece * lane : (piece + 1) * lane] * counts[group : group + 1, :]
-            pieces = parts(weighted, 3)
-            ones = jnp.ones((16, lane), jnp.bfloat16)
-            spread = lax.dot_general(ones, pieces, CONTRACT_LAST, preferred_element_type=jnp.float32)
-            terms = spread[:8, :loads] + spread[:8, loads : 2 * loads] + spread[:8, 2 * loads :]
-            own_bal[:, :loads] = terms
-            own_bal[:, loads:] = jnp.zeros((8, own_bal.shape[1] - loads), jnp.float32)
-            bal_sums[me_b] = own_bal[...]
-            for step in range(1, n_bal):
-                pltpu.make_async_remote_copy(
-                    src_ref=own_bal, dst_ref=bal_sums.at[me_b],
-                    send_sem=bal_send.at[step], recv_sem=bal_recv.at[step],
-                    device_id={"bal": lax.rem(me_b + step, n_bal)}, device_id_type=MESH,
-                ).start()
-
-        projected = parts(running[:loads] + running[loads:], 2)
+    def apply(turn, half, running):
+        projected = parts(running[:part] + running[part:], 2)
         for face in SEND_ORDER:
             stacked = jnp.dot(projected, kept[:, span(face)], preferred_element_type=jnp.float32)
-            send[turn, face] = (
-                stacked[:loads] + stacked[loads:] + direction[:, span(face)] * diag[0:1, span(face)]
+            send[turn, half, face] = (
+                stacked[:part] + stacked[part:] + direction[lines(half), span(face)] * diag[0:1, span(face)]
             )
-            start_face(turn, face)
-
-        if last:
-            for step in range(1, n_bal):
-                source = lax.rem(me_b + n_bal - step, n_bal)
-                pltpu.make_async_remote_copy(
-                    src_ref=own_bal, dst_ref=bal_sums.at[source],
-                    send_sem=bal_send.at[step], recv_sem=bal_recv.at[step],
-                    device_id={"bal": source}, device_id_type=MESH,
-                ).wait()
-            summed = bal_sums[0]
-            for index in range(1, n_bal):
-                summed = summed + bal_sums[index]
-            own_space[...] = summed
-            space_sums[me_s] = summed
-            for step in range(1, n_space):
-                pltpu.make_async_remote_copy(
-                    src_ref=own_space, dst_ref=space_sums.at[me_s],
-                    send_sem=space_send.at[step], recv_sem=space_recv.at[step],
-                    device_id={"space": lax.rem(me_s + step, n_space)}, device_id_type=MESH,
-                ).start()
-            solution_copy = pltpu.make_async_copy(solution_ref, solution_hbm, output_sem.at[0])
-            solution_copy.start()
-            for face in WAIT_ORDER:
-                wait_face(turn, face)
-                final = residual[:, span(face)] - (send[turn, face] + recv[turn, face])
-                residual_ref[:, span(face)] = product(final, turned[face], CONTRACT_MIDDLE)
-        else:
-            rho_next = 1.0 / (2.0 * ratio_c - cheb_rho)
+            start_face(turn, half, face)
+
+    for half in range(HALVES):
+        running = None
+        for face in WAIT_ORDER:
+            wait_face(0, half, face)
+            first = send[0, half, face] + recv[0, half, face]
+            residual[lines(half), span(face)] = first
+            direction[lines(half), span(face)] = first / center
+            total[lines(half), span(face)] = first / center
+            running = project(half, face, running)
+        apply(1, half, running)
+
+    def weigh(half):
+        weighted = jnp.zeros((part, lane), jnp.float32)
+        for face in range(FACES):
+            local = product(total[lines(half), span(face)], turned[face], CONTRACT_MIDDLE)
+            solution_ref[lines(half), span(face)] = local
+            negative = jnp.minimum(local, 0.0)
+            squares = negative * negative
+            for piece in range(face_len // lane):
+                group = face * (face_len // lane) + piece
+                weighted = weighted + squares[:, piece * lane : (piece + 1) * lane] * counts[group : group + 1, :]
+        violated[lines(half), :] = weighted
+
+    cheb_rho = 1.0 / ratio_c
+    for turn in range(1, ITERS):
+        rho_next = 1.0 / (2.0 * ratio_c - cheb_rho)
+        for half in range(HALVES):
             running = None
             for face in WAIT_ORDER:
-                wait_face(turn, face)
-                updated = residual[:, span(face)] - (send[turn, face] + recv[turn, face])
-                residual[:, span(face)] = updated
-                moved = rho_next * cheb_rho * direction[:, span(face)] + 2.0 * rho_next / half_span * updated
-                direction[:, span(face)] = moved
-                total[:, span(face)] = total[:, span(face)] + moved
-                running = project(face, running)
-            cheb_rho = rho_next
-
-    residual_copy = pltpu.make_async_copy(residual_ref, residual_hbm, output_sem.at[1])
-    residual_copy.start()
+                wait_face(turn, half, face)
+                updated = residual[lines(half), span(face)] - (send[turn, half, face] + recv[turn, half, face])
+                residual[lines(half), span(face)] = updated
+                moved = (
+                    rho_next * cheb_rho * direction[lines(half), span(face)] + 2.0 * rho_next / half_span * updated
+                )
+                direction[lines(half), span(face)] = moved
+                total[lines(half), span(face)] = total[lines(half), span(face)] + moved
+                running = project(half, face, running)
+            apply(turn + 1, half, running)
+            if turn + 1 == ITERS:
+                weigh(half)
+        cheb_rho = rho_next
+
+    pieces = parts(violated[...], 3)
+    ones = jnp.ones((16, lane), jnp.bfloat16)
+    spread = lax.dot_general(ones, pieces, CONTRACT_LAST, preferred_element_type=jnp.float32)
+    terms = spread[:8, :loads] + spread[:8, loads : 2 * loads] + spread[:8, 2 * loads :]
+    own_bal[:, loads:] = jnp.zeros((8, own_bal.shape[1] - loads), jnp.float32)
+    own_bal[:, :loads] = terms
+    bal_sums[me_b] = own_bal[...]
+    for step in range(1, n_bal):
+        pltpu.make_async_remote_copy(
+            src_ref=own_bal, dst_ref=bal_sums.at[me_b],
+            send_sem=bal_send.at[step], recv_sem=bal_recv.at[step],
+            device_id={"bal": lax.rem(me_b + step, n_bal)}, device_id_type=MESH,
+        ).start()
+    solution_copy = pltpu.make_async_copy(solution_ref, solution_hbm, output_sem.at[0])
+    solution_copy.start()
+
+    def settle(half):
+        for face in WAIT_ORDER:
+            wait_face(ITERS, half, face)
+            final = residual[lines(half), span(face)] - (send[ITERS, half, face] + recv[ITERS, half, face])
+            residual_ref[lines(half), span(face)] = product(final, turned[face], CONTRACT_MIDDLE)
+        copy = pltpu.make_async_copy(
+            residual_ref.at[lines(half)], residual_hbm.at[lines(half)], output_sem.at[2 + half]
+        )
+        copy.start()
+        return copy
+
+    residual_copies = [settle(0)]
+
+    for step in range(1, n_bal):
+        source = lax.rem(me_b + n_bal - step, n_bal)
+        pltpu.make_async_remote_copy(
+            src_ref=own_bal, dst_ref=bal_sums.at[source],
+            send_sem=bal_send.at[step], recv_sem=bal_recv.at[step],
+            device_id={"bal": source}, device_id_type=MESH,
+        ).wait()
+    summed = bal_sums[0]
+    for index in range(1, n_bal):
+        summed = summed + bal_sums[index]
+    own_space[...] = summed
+    space_sums[me_s] = summed
+    for step in range(1, n_space):
+        pltpu.make_async_remote_copy(
+            src_ref=own_space, dst_ref=space_sums.at[me_s],
+            send_sem=space_send.at[step], recv_sem=space_recv.at[step],
+            device_id={"space": lax.rem(me_s + step, n_space)}, device_id_type=MESH,
+        ).start()
+
+    for half in range(1, HALVES):
+        residual_copies.append(settle(half))
+
     for step in range(1, n_space):
         source = lax.rem(me_s + n_space - step, n_space)
         pltpu.make_async_remote_copy(
@@ -270,28 +298,45 @@
     for index in range(1, n_space):
         summed = summed + space_sums[index]
     violation_ref[...] = jnp.sqrt(summed[0:1, :loads] + 1e-06)
-    violation_copy = pltpu.make_async_copy(violation_ref, violation_hbm, output_sem.at[2])
+    violation_copy = pltpu.make_async_copy(violation_ref, violation_hbm, output_sem.at[1])
     violation_copy.start()
 
     for turn in range(ITERS + 1):
         for face in range(FACES):
             @pl.when(present[face])
             def _():
-                face_copy(turn, face).wait_send()
+                for half in range(HALVES):
+                    face_copy(turn, half, face).wait_send()
     solution_copy.wait()
-    residual_copy.wait()
     violation_copy.wait()
-
-
-def finish(solution_in, residual_in, violation_in, solution_out, residual_out, violation_out, sems):
-    pairs = ((solution_in, solution_out), (residual_in, residual_out), (violation_in, violation_out))
-    copies = [
-        pltpu.make_async_copy(source, target, sems.at[index]) for index, (source, target) in enumerate(pairs)
+    for copy in residual_copies:
+        copy.wait()
+
+
+def finish(
+    solution_in, residual_in, violation_in, solution_out, residual_out, violation_out,
+    solution_held, residual_held, violation_held, in_sems, out_sems,
+):
+    rows = solution_held.shape[0]
+    part = rows // HALVES
+    moves = [(violation_in, violation_held, violation_out)]
+    for half in range(HALVES):
+        span = slice(half * part, (half + 1) * part)
+        moves.append((residual_in.at[span], residual_held.at[span], residual_out.at[span]))
+        moves.append((solution_in.at[span], solution_held.at[span], solution_out.at[span]))
+    fetches = [
+        pltpu.make_async_copy(source, held, in_sems.at[index]) for index, (source, held, _) in enumerate(moves)
     ]
-    for copy in copies:
-        copy.start()
-    for copy in copies:
-        copy.wait()
+    stores = [
+        pltpu.make_async_copy(held, target, out_sems.at[index]) for index, (_, held, target) in enumerate(moves)
+    ]
+    for fetch in fetches:
+        fetch.start()
+    for fetch, store in zip(fetches, stores):
+        fetch.wait()
+        store.start()
+    for store in stores:
+        store.wait()
 
 
 def local(n_space, n_bal, panels, enrich, compliance, loads, face_maps, face_lengths, contact):
@@ -330,16 +375,17 @@
             pltpu.VMEM(field, jnp.float32),
             pltpu.VMEM(field, jnp.float32),
             pltpu.VMEM(field, jnp.float32),
-            pltpu.VMEM((turns, FACES, n_loads, face_len), jnp.float32),
-            pltpu.VMEM((turns, FACES, n_loads, face_len), jnp.float32),
+            pltpu.VMEM((n_loads, 128), jnp.float32),
+            pltpu.VMEM((turns, HALVES, FACES, n_loads // HALVES, face_len), jnp.float32),
+            pltpu.VMEM((turns, HALVES, FACES, n_loads // HALVES, face_len), jnp.float32),
             pltpu.VMEM((n_bal, 8, width), jnp.float32),
             pltpu.VMEM((n_space, 8, width), jnp.float32),
             pltpu.VMEM((8, width), jnp.float32),
             pltpu.VMEM((8, width), jnp.float32),
             pltpu.SemaphoreType.DMA((6,)),
-            pltpu.SemaphoreType.DMA((3,)),
-            pltpu.SemaphoreType.DMA((turns, FACES)),
-            pltpu.SemaphoreType.DMA((turns, FACES)),
+            pltpu.SemaphoreType.DMA((2 + HALVES,)),
+            pltpu.SemaphoreType.DMA((turns, HALVES, FACES)),
+            pltpu.SemaphoreType.DMA((turns, HALVES, FACES)),
             pltpu.SemaphoreType.DMA((n_bal,)),
             pltpu.SemaphoreType.DMA((n_bal,)),
             pltpu.SemaphoreType.DMA((n_space,)),
@@ -364,7 +410,13 @@
         ),
         in_specs=[hbm] * 3,
         out_specs=(hbm, hbm, hbm),
-        scratch_shapes=[pltpu.SemaphoreType.DMA((3,))],
+        scratch_shapes=[
+            pltpu.VMEM(field, jnp.float32),
+            pltpu.VMEM(field, jnp.float32),
+            pltpu.VMEM((1, n_loads), jnp.float32),
+            pltpu.SemaphoreType.DMA((1 + 2 * HALVES,)),
+            pltpu.SemaphoreType.DMA((1 + 2 * HALVES,)),
+        ],
         compiler_params=pltpu.CompilerParams(vmem_limit_bytes=VMEM_BYTES),
         name="finish",
     )(*out)

time: 45.3 us -> 31.9 us (0.70)
  Pallas kernels: 43.8 us -> 30.4 us
    pallas_call x1, Pallas kernels: 17 us -> 1.84 us  [local(): pl.pallas_call(finish, out_shape=(jax.ShapeDtypeStruct(field, jnp.float32...]
    pallas_call x1, Pallas kernels: 26.8 us -> 28.6 us  [local(): pl.pallas_call(functools.partial(kernel, n_space, n_bal), out_shape=(jax....]
where the time goes in v3:
time: 31.9 us; the launch traced here: 31.7 us
  Pallas kernels  30.4 us (95%)
  between operations  1.29 us (4%)
    pallas_call x1, Pallas kernels, local(): pl.pallas_call(functools.partial(kernel, n_space, n_bal), out_shape=(jax....  28.6 us
    pallas_call x1, Pallas kernels, local(): pl.pallas_call(finish, out_shape=(jax.ShapeDtypeStruct(field, jnp.float32...  1.84 us

profile of v3, /device:TPU:0, one launch (start us, length us, event | category | flops | bytes accessed | tf_op | source)
XLA Modules:
  0.0 31.7 jit_solution(216771156791808292)
XLA Ops:
  1.3 28.6 %feti.1 = (f32[64,1024]{1,0:T(8,128)}, f32[64,1024]{1,0:T(8,128)}, f32[1,64]{1,0:T(1,128)}) custom-call(s32[1,4]{1,0:T(1,128)} %bitcast.15, s32[1,1]{1,0:T(1,128)S(6)} %copy.10.enrich_ref, s32[4,256]{1,0:T(4,128)} %bitcast.13, f32[1,1024]{1,0:T(1,128)} %bitcast.14, s32[1,128]{1,0:T(1,128)} %bitcast.16, f32[64,1024]{1,0:T(8,128)} %bitcast.10, ...), custom_call_target="tpu_custom_call" | custom-call | flops 2147483648 | bytes 2883584 | tf_op jit(solution)/shard_map/feti/pallas_call | solution.py:351
  29.9 1.8 %finish.1 = (f32[64,1024]{1,0:T(8,128)}, f32[64,1024]{1,0:T(8,128)}, f32[1,64]{1,0:T(1,128)}) custom-call(f32[64,1024]{1,0:T(8,128)} %get-tuple-element.9.solution_in, f32[64,1024]{1,0:T(8,128)} %get-tuple-element.10.residual_in, f32[1,64]{1,0:T(1,128)} %get-tuple-element.11.violation_in), custom_call_target="tpu_custom_call" | custom-call | tf_op jit(solution)/shard_map/finish/pallas_call | solution.py:404

commit v4 on v3

--- a/solution.py
+++ b/solution.py
@@ -11,10 +11,10 @@
 BLOCK_ROWS = 512
 ITERS = 3
 FACES = 4
-HALVES = 2
+HALVES = 1
 VMEM_BYTES = 64 * 1024 * 1024
-SEND_ORDER = (0, 1, 2, 3)
-WAIT_ORDER = (2, 3, 0, 1)
+SPACE_PAIR = (0, 1)
+BAL_PAIR = (2, 3)
 MESH = pl.DeviceIdType.MESH
 CONTRACT_LAST = (((1,), (1,)), ((), ()))
 CONTRACT_MIDDLE = (((1,), (0,)), ((), ()))
@@ -55,7 +55,7 @@
     lengths_hbm, enrich_ref, maps_hbm, compliance_hbm, contact_hbm, loads_hbm, panel_hbm,
     solution_hbm, residual_hbm, violation_hbm,
     lengths_ref, maps_ref, compliance_ref, contact_ref, loads_ref,
-    solution_ref, residual_ref, violation_ref, turned, panel, kept, kept_turned, onehot, diag, direction, total, residual, violated, send, recv, bal_sums, space_sums, own_bal, own_space,
+    solution_ref, residual_ref, violation_ref, turned, panel, kept, kept_turned, onehot, diag, weights, direction, total, residual, violated, send, recv, bal_sums, space_sums, own_bal, own_space,
     input_sem, output_sem, send_sem, recv_sem, bal_send, bal_recv, space_send, space_recv,
 ):
     me_s = lax.axis_index("space")
@@ -131,14 +131,14 @@
         onehot[face] = jnp.where(hit, 1.0, 0.0).astype(jnp.bfloat16)
 
     copies[2].wait()
-    for face in SEND_ORDER:
+    for face in SPACE_PAIR + BAL_PAIR:
         canonical = product(loads_ref[:, span(face)], onehot[face], CONTRACT_MIDDLE)
         for half in range(HALVES):
             send[0, half, face] = canonical[lines(half)]
 
     pl.semaphore_wait(barrier, n_bal - 1 + n_space - 1)
     for half in range(HALVES):
-        for face in SEND_ORDER:
+        for face in SPACE_PAIR + BAL_PAIR:
             start_face(0, half, face)
 
     for face in range(FACES):
@@ -168,6 +168,17 @@
         preferred_element_type=jnp.float32,
     )
 
+    per_face = face_len // lane
+    for face in range(FACES):
+        weight = jnp.zeros((16, face_len), jnp.float32)
+        for piece in range(per_face):
+            group = face * per_face + piece
+            row = jnp.broadcast_to(counts[group : group + 1, :], (16, lane)).astype(jnp.bfloat16)
+            weight = weight + jnp.dot(
+                row, onehot[face, piece * lane : (piece + 1) * lane, :], preferred_element_type=jnp.float32
+            )
+        weights[:, span(face)] = weight
+
     copies[3].wait()
     live_rows = enrich_ref[0, 0] * BLOCK_ROWS
     keep = lax.broadcasted_iota(jnp.int32, (rows, face_len), 0) < live_rows
@@ -177,93 +188,107 @@
         kept[:, span(face)] = masked
         kept_turned[span(face), :] = masked.T
 
-    def project(half, face, running):
+    def pair_span(pair):
+        return slice(pair[0] * face_len, (pair[-1] + 1) * face_len)
+
+    def project(half, pair, running):
         term = jnp.dot(
-            parts(direction[lines(half), span(face)], 2), kept_turned[span(face), :],
+            parts(direction[lines(half), pair_span(pair)], 2), kept_turned[pair_span(pair), :],
             preferred_element_type=jnp.float32,
         )
         return term if running is None else running + term
 
     def apply(turn, half, running):
         projected = parts(running[:part] + running[part:], 2)
-        for face in SEND_ORDER:
-            stacked = jnp.dot(projected, kept[:, span(face)], preferred_element_type=jnp.float32)
-            send[turn, half, face] = (
-                stacked[:part] + stacked[part:] + direction[lines(half), span(face)] * diag[0:1, span(face)]
+        for pair in (SPACE_PAIR, BAL_PAIR):
+            stacked = jnp.dot(projected, kept[:, pair_span(pair)], preferred_element_type=jnp.float32)
+            image = (
+                stacked[:part] + stacked[part:]
+                + direction[lines(half), pair_span(pair)] * diag[0:1, pair_span(pair)]
             )
-            start_face(turn, half, face)
+            for index, face in enumerate(pair):
+                send[turn, half, face] = image[:, index * face_len : (index + 1) * face_len]
+            for face in pair:
+                start_face(turn, half, face)
+
+    def share_violation():
+        pieces = parts(violated[...], 3)
+        ones = jnp.ones((16, lane), jnp.bfloat16)
+        spread = lax.dot_general(ones, pieces, CONTRACT_LAST, preferred_element_type=jnp.float32)
+        terms = spread[:8, :loads] + spread[:8, loads : 2 * loads] + spread[:8, 2 * loads :]
+        own_bal[:, loads:] = jnp.zeros((8, own_bal.shape[1] - loads), jnp.float32)
+        own_bal[:, :loads] = terms
+        bal_sums[me_b] = own_bal[...]
+        for step in range(1, n_bal):
+            pltpu.make_async_remote_copy(
+                src_ref=own_bal, dst_ref=bal_sums.at[me_b],
+                send_sem=bal_send.at[step], recv_sem=bal_recv.at[step],
+                device_id={"bal": lax.rem(me_b + step, n_bal)}, device_id_type=MESH,
+            ).start()
 
     for half in range(HALVES):
         running = None
-        for face in WAIT_ORDER:
-            wait_face(0, half, face)
-            first = send[0, half, face] + recv[0, half, face]
-            residual[lines(half), span(face)] = first
-            direction[lines(half), span(face)] = first / center
-            total[lines(half), span(face)] = first / center
-            running = project(half, face, running)
+        for pair in (BAL_PAIR, SPACE_PAIR):
+            for face in pair:
+                wait_face(0, half, face)
+            for face in pair:
+                first = send[0, half, face] + recv[0, half, face]
+                residual[lines(half), span(face)] = first
+                direction[lines(half), span(face)] = first * (1.0 / center)
+                total[lines(half), span(face)] = first * (1.0 / center)
+            running = project(half, pair, running)
         apply(1, half, running)
-
-    def weigh(half):
-        weighted = jnp.zeros((part, lane), jnp.float32)
-        for face in range(FACES):
-            local = product(total[lines(half), span(face)], turned[face], CONTRACT_MIDDLE)
-            solution_ref[lines(half), span(face)] = local
-            negative = jnp.minimum(local, 0.0)
-            squares = negative * negative
-            for piece in range(face_len // lane):
-                group = face * (face_len // lane) + piece
-                weighted = weighted + squares[:, piece * lane : (piece + 1) * lane] * counts[group : group + 1, :]
-        violated[lines(half), :] = weighted
 
     cheb_rho = 1.0 / ratio_c
     for turn in range(1, ITERS):
         rho_next = 1.0 / (2.0 * ratio_c - cheb_rho)
         for half in range(HALVES):
             running = None
-            for face in WAIT_ORDER:
-                wait_face(turn, half, face)
-                updated = residual[lines(half), span(face)] - (send[turn, half, face] + recv[turn, half, face])
-                residual[lines(half), span(face)] = updated
-                moved = (
-                    rho_next * cheb_rho * direction[lines(half), span(face)] + 2.0 * rho_next / half_span * updated
-                )
-                direction[lines(half), span(face)] = moved
-                total[lines(half), span(face)] = total[lines(half), span(face)] + moved
-                running = project(half, face, running)
+            weighted = jnp.zeros((part, face_len), jnp.float32)
+            for pair in (BAL_PAIR, SPACE_PAIR):
+                for face in pair:
+                    wait_face(turn, half, face)
+                for face in pair:
+                    updated = residual[lines(half), span(face)] - (send[turn, half, face] + recv[turn, half, face])
+                    residual[lines(half), span(face)] = updated
+                    moved = (
+                        rho_next * cheb_rho * direction[lines(half), span(face)]
+                        + 2.0 * rho_next / half_span * updated
+                    )
+                    direction[lines(half), span(face)] = moved
+                    summed = total[lines(half), span(face)] + moved
+                    total[lines(half), span(face)] = summed
+                    negative = jnp.minimum(summed, 0.0)
+                    weighted = weighted + negative * negative * weights[0:1, span(face)]
+                running = project(half, pair, running)
+            if turn + 1 == ITERS:
+                narrow = weighted[:, :lane]
+                for piece in range(1, per_face):
+                    narrow = narrow + weighted[:, piece * lane : (piece + 1) * lane]
+                violated[lines(half), :] = narrow
+                if half + 1 == HALVES:
+                    share_violation()
             apply(turn + 1, half, running)
-            if turn + 1 == ITERS:
-                weigh(half)
         cheb_rho = rho_next
 
-    pieces = parts(violated[...], 3)
-    ones = jnp.ones((16, lane), jnp.bfloat16)
-    spread = lax.dot_general(ones, pieces, CONTRACT_LAST, preferred_element_type=jnp.float32)
-    terms = spread[:8, :loads] + spread[:8, loads : 2 * loads] + spread[:8, 2 * loads :]
-    own_bal[:, loads:] = jnp.zeros((8, own_bal.shape[1] - loads), jnp.float32)
-    own_bal[:, :loads] = terms
-    bal_sums[me_b] = own_bal[...]
-    for step in range(1, n_bal):
-        pltpu.make_async_remote_copy(
-            src_ref=own_bal, dst_ref=bal_sums.at[me_b],
-            send_sem=bal_send.at[step], recv_sem=bal_recv.at[step],
-            device_id={"bal": lax.rem(me_b + step, n_bal)}, device_id_type=MESH,
-        ).start()
+    for face in range(FACES):
+        solution_ref[:, span(face)] = product(total[:, span(face)], turned[face], CONTRACT_MIDDLE)
     solution_copy = pltpu.make_async_copy(solution_ref, solution_hbm, output_sem.at[0])
     solution_copy.start()
 
     def settle(half):
-        for face in WAIT_ORDER:
-            wait_face(ITERS, half, face)
-            final = residual[lines(half), span(face)] - (send[ITERS, half, face] + recv[ITERS, half, face])
-            residual_ref[lines(half), span(face)] = product(final, turned[face], CONTRACT_MIDDLE)
+        for pair in (BAL_PAIR, SPACE_PAIR):
+            for face in pair:
+                wait_face(ITERS, half, face)
+            for face in pair:
+                final = residual[lines(half), span(face)] - (send[ITERS, half, face] + recv[ITERS, half, face])
+                residual_ref[lines(half), span(face)] = product(final, turned[face], CONTRACT_MIDDLE)
         copy = pltpu.make_async_copy(
             residual_ref.at[lines(half)], residual_hbm.at[lines(half)], output_sem.at[2 + half]
         )
         copy.start()
         return copy
 
-    residual_copies = [settle(0)]
 
     for step in range(1, n_bal):
         source = lax.rem(me_b + n_bal - step, n_bal)
@@ -284,8 +309,7 @@
             device_id={"space": lax.rem(me_s + step, n_space)}, device_id_type=MESH,
         ).start()
 
-    for half in range(1, HALVES):
-        residual_copies.append(settle(half))
+    residual_copies = [settle(half) for half in range(HALVES)]
 
     for step in range(1, n_space):
         source = lax.rem(me_s + n_space - step, n_space)
@@ -371,6 +395,7 @@
             pltpu.VMEM((rows, columns), jnp.bfloat16),
             pltpu.VMEM((rows, columns), jnp.bfloat16),
             pltpu.VMEM((FACES, face_len, face_len), jnp.bfloat16),
+            pltpu.VMEM((16, columns), jnp.float32),
             pltpu.VMEM((16, columns), jnp.float32),
             pltpu.VMEM(field, jnp.float32),
             pltpu.VMEM(field, jnp.float32),

time: 31.9 us -> 29.1 us (0.912)
  Pallas kernels: 30.4 us -> 27.6 us
    pallas_call x1, Pallas kernels: 28.6 us -> 25.8 us  [local(): pl.pallas_call(functools.partial(kernel, n_space, n_bal), out_shape=(jax....]
where the time goes in v4:
time: 29.1 us; the launch traced here: 28.9 us
  Pallas kernels  27.6 us (95%)
  between operations  1.29 us (4%)
    pallas_call x1, Pallas kernels, local(): pl.pallas_call(functools.partial(kernel, n_space, n_bal), out_shape=(jax....  25.8 us
    pallas_call x1, Pallas kernels, local(): pl.pallas_call(finish, out_shape=(jax.ShapeDtypeStruct(field, jnp.float32...  1.79 us

profile of v4, /device:TPU:0, one launch (start us, length us, event | category | flops | bytes accessed | tf_op | source)
XLA Modules:
  0.0 28.9 jit_solution(16744332404497766957)
XLA Ops:
  1.3 25.8 %feti.1 = (f32[64,1024]{1,0:T(8,128)}, f32[64,1024]{1,0:T(8,128)}, f32[1,64]{1,0:T(1,128)}) custom-call(s32[1,4]{1,0:T(1,128)} %bitcast.15, s32[1,1]{1,0:T(1,128)S(6)} %copy.10.enrich_ref, s32[4,256]{1,0:T(4,128)} %bitcast.13, f32[1,1024]{1,0:T(1,128)} %bitcast.14, s32[1,128]{1,0:T(1,128)} %bitcast.16, f32[64,1024]{1,0:T(8,128)} %bitcast.10, ...), custom_call_target="tpu_custom_call" | custom-call | flops 2147483648 | bytes 2883584 | tf_op jit(solution)/shard_map/feti/pallas_call | solution.py:375
  27.1 1.8 %finish.1 = (f32[64,1024]{1,0:T(8,128)}, f32[64,1024]{1,0:T(8,128)}, f32[1,64]{1,0:T(1,128)}) custom-call(f32[64,1024]{1,0:T(8,128)} %get-tuple-element.9.solution_in, f32[64,1024]{1,0:T(8,128)} %get-tuple-element.10.residual_in, f32[1,64]{1,0:T(1,128)} %get-tuple-element.11.violation_in), custom_call_target="tpu_custom_call" | custom-call | tf_op jit(solution)/shard_map/finish/pallas_call | solution.py:429

commit v5 on v4

--- a/solution.py
+++ b/solution.py
@@ -125,59 +125,64 @@
     copies[1].wait()
     row_of = lax.broadcasted_iota(jnp.int32, (face_len, face_len), 0)
     slot_of = lax.broadcasted_iota(jnp.int32, (face_len, face_len), 1)
-    for face in range(FACES):
-        table = jnp.broadcast_to(maps_ref[face : face + 1, :], (face_len, face_len))
-        hit = (row_of == table) & (slot_of < lengths_ref[0, face])
-        onehot[face] = jnp.where(hit, 1.0, 0.0).astype(jnp.bfloat16)
-
-    copies[2].wait()
-    for face in SPACE_PAIR + BAL_PAIR:
-        canonical = product(loads_ref[:, span(face)], onehot[face], CONTRACT_MIDDLE)
+    for pair in (SPACE_PAIR, BAL_PAIR):
+        for face in pair:
+            table = jnp.broadcast_to(maps_ref[face : face + 1, :], (face_len, face_len))
+            hit = (row_of == table) & (slot_of < lengths_ref[0, face])
+            onehot[face] = jnp.where(hit, 1.0, 0.0).astype(jnp.bfloat16)
+        if pair == SPACE_PAIR:
+            copies[2].wait()
+        for face in pair:
+            canonical = product(loads_ref[:, span(face)], onehot[face], CONTRACT_MIDDLE)
+            for half in range(HALVES):
+                send[0, half, face] = canonical[lines(half)]
+        if pair == SPACE_PAIR:
+            pl.semaphore_wait(barrier, n_bal - 1 + n_space - 1)
         for half in range(HALVES):
-            send[0, half, face] = canonical[lines(half)]
-
-    pl.semaphore_wait(barrier, n_bal - 1 + n_space - 1)
-    for half in range(HALVES):
-        for face in SPACE_PAIR + BAL_PAIR:
-            start_face(0, half, face)
-
-    for face in range(FACES):
-        @pl.when(jnp.logical_not(present[face]))
-        def _():
-            for turn in range(ITERS + 1):
-                for half in range(HALVES):
-                    recv[turn, half, face] = jnp.zeros((part, face_len), jnp.float32)
+            for face in pair:
+                start_face(0, half, face)
+
+    def clear(turns):
+        for face in range(FACES):
+            @pl.when(jnp.logical_not(present[face]))
+            def _():
+                for turn in turns:
+                    for half in range(HALVES):
+                        recv[turn, half, face] = jnp.zeros((part, face_len), jnp.float32)
+
+    clear((0,))
+
+    lane = 128
+    per_face = face_len // lane
+    groups = columns // lane
+
+    def prepare_weights():
+        contact = contact_ref[...]
+        group_rows = max(groups, 8)
+        group_of = lax.broadcasted_iota(jnp.int32, (group_rows, contact.shape[1]), 0)
+        place_of = lax.broadcasted_iota(jnp.int32, (lane, contact.shape[1]), 0)
+        in_group = jnp.where(group_of == lax.shift_right_logical(contact, 7), 1.0, 0.0)
+        at_place = jnp.where(place_of == (contact & (lane - 1)), 1.0, 0.0)
+        counts = lax.dot_general(
+            in_group.astype(jnp.bfloat16), at_place.astype(jnp.bfloat16), CONTRACT_LAST,
+            preferred_element_type=jnp.float32,
+        )
+        for face in range(FACES):
+            turned[face] = onehot[face].T
+            weight = jnp.zeros((16, face_len), jnp.float32)
+            for piece in range(per_face):
+                group = face * per_face + piece
+                row = jnp.broadcast_to(counts[group : group + 1, :], (16, lane)).astype(jnp.bfloat16)
+                weight = weight + jnp.dot(
+                    row, onehot[face, piece * lane : (piece + 1) * lane, :], preferred_element_type=jnp.float32
+                )
+            weights[:, span(face)] = weight
 
     for index in range(4, len(copies)):
         copies[index].wait()
     for face in range(FACES):
-        turned[face] = onehot[face].T
         wide = jnp.broadcast_to(compliance_ref[:, span(face)], (16, face_len))
         diag[:, span(face)] = product(wide, onehot[face], CONTRACT_MIDDLE, 3)
-
-    lane = 128
-    contact = contact_ref[...]
-    groups = columns // lane
-    group_rows = max(groups, 8)
-    group_of = lax.broadcasted_iota(jnp.int32, (group_rows, contact.shape[1]), 0)
-    place_of = lax.broadcasted_iota(jnp.int32, (lane, contact.shape[1]), 0)
-    in_group = jnp.where(group_of == lax.shift_right_logical(contact, 7), 1.0, 0.0)
-    at_place = jnp.where(place_of == (contact & (lane - 1)), 1.0, 0.0)
-    counts = lax.dot_general(
-        in_group.astype(jnp.bfloat16), at_place.astype(jnp.bfloat16), CONTRACT_LAST,
-        preferred_element_type=jnp.float32,
-    )
-
-    per_face = face_len // lane
-    for face in range(FACES):
-        weight = jnp.zeros((16, face_len), jnp.float32)
-        for piece in range(per_face):
-            group = face * per_face + piece
-            row = jnp.broadcast_to(counts[group : group + 1, :], (16, lane)).astype(jnp.bfloat16)
-            weight = weight + jnp.dot(
-                row, onehot[face, piece * lane : (piece + 1) * lane, :], preferred_element_type=jnp.float32
-            )
-        weights[:, span(face)] = weight
 
     copies[3].wait()
     live_rows = enrich_ref[0, 0] * BLOCK_ROWS
@@ -238,6 +243,9 @@
                 total[lines(half), span(face)] = first * (1.0 / center)
             running = project(half, pair, running)
         apply(1, half, running)
+
+    clear(range(1, ITERS + 1))
+    prepare_weights()
 
     cheb_rho = 1.0 / ratio_c
     for turn in range(1, ITERS):

time: 29.1 us -> 29.2 us (level)
  no operation moved by 1% of the time
where the time goes in v5:
time: 29.2 us; the launch traced here: 29 us
  Pallas kernels  27.7 us (95%)
  between operations  1.29 us (4%)
    pallas_call x1, Pallas kernels, local(): pl.pallas_call(functools.partial(kernel, n_space, n_bal), out_shape=(jax....  25.9 us
    pallas_call x1, Pallas kernels, local(): pl.pallas_call(finish, out_shape=(jax.ShapeDtypeStruct(field, jnp.float32...  1.79 us

profile of v5, /device:TPU:0, one launch (start us, length us, event | category | flops | bytes accessed | tf_op | source)
XLA Modules:
  0.0 29.0 jit_solution(10735705416059911560)
XLA Ops:
  1.3 25.9 %feti.1 = (f32[64,1024]{1,0:T(8,128)}, f32[64,1024]{1,0:T(8,128)}, f32[1,64]{1,0:T(1,128)}) custom-call(s32[1,4]{1,0:T(1,128)} %bitcast.15, s32[1,1]{1,0:T(1,128)S(6)} %copy.10.enrich_ref, s32[4,256]{1,0:T(4,128)} %bitcast.13, f32[1,1024]{1,0:T(1,128)} %bitcast.14, s32[1,128]{1,0:T(1,128)} %bitcast.16, f32[64,1024]{1,0:T(8,128)} %bitcast.10, ...), custom_call_target="tpu_custom_call" | custom-call | flops 2147483648 | bytes 2883584 | tf_op jit(solution)/shard_map/feti/pallas_call | solution.py:383
  27.2 1.8 %finish.1 = (f32[64,1024]{1,0:T(8,128)}, f32[64,1024]{1,0:T(8,128)}, f32[1,64]{1,0:T(1,128)}) custom-call(f32[64,1024]{1,0:T(8,128)} %get-tuple-element.9.solution_in, f32[64,1024]{1,0:T(8,128)} %get-tuple-element.10.residual_in, f32[1,64]{1,0:T(1,128)} %get-tuple-element.11.violation_in), custom_call_target="tpu_custom_call" | custom-call | tf_op jit(solution)/shard_map/finish/pallas_call | solution.py:437

commit v6 on v5

--- a/solution.py
+++ b/solution.py
@@ -55,7 +55,7 @@
     lengths_hbm, enrich_ref, maps_hbm, compliance_hbm, contact_hbm, loads_hbm, panel_hbm,
     solution_hbm, residual_hbm, violation_hbm,
     lengths_ref, maps_ref, compliance_ref, contact_ref, loads_ref,
-    solution_ref, residual_ref, violation_ref, turned, panel, kept, kept_turned, onehot, diag, weights, direction, total, residual, violated, send, recv, bal_sums, space_sums, own_bal, own_space,
+    solution_ref, residual_ref, violation_ref, turned, panel, kept, kept_turned, gram_high, gram_low, onehot, diag, weights, direction, total, residual, violated, send, recv, bal_sums, space_sums, own_bal, own_space,
     input_sem, output_sem, send_sem, recv_sem, bal_send, bal_recv, space_send, space_recv,
 ):
     me_s = lax.axis_index("space")
@@ -245,7 +245,26 @@
         apply(1, half, running)
 
     clear(range(1, ITERS + 1))
-    prepare_weights()
+
+    for face in range(FACES):
+        gram = jnp.dot(kept_turned[...], kept[:, span(face)], preferred_element_type=jnp.float32)
+        high = gram.astype(jnp.bfloat16)
+        gram_high[:, span(face)] = high
+        gram_low[:, span(face)] = (gram - high.astype(jnp.float32)).astype(jnp.bfloat16)
+
+    def multiply(half, pair, running):
+        stacked = parts(direction[lines(half), pair_span(pair)], 2)
+        term = jnp.dot(stacked, gram_high[pair_span(pair), :], preferred_element_type=jnp.float32)
+        small = jnp.dot(stacked[:part], gram_low[pair_span(pair), :], preferred_element_type=jnp.float32)
+        term = term[:part] + term[part:] + small
+        return term if running is None else running + term
+
+    def send_image(turn, half, product_rows):
+        image = product_rows + direction[lines(half), :] * diag[0:1, :]
+        for face in range(FACES):
+            send[turn, half, face] = image[:, span(face)]
+        for face in SPACE_PAIR + BAL_PAIR:
+            start_face(turn, half, face)
 
     cheb_rho = 1.0 / ratio_c
     for turn in range(1, ITERS):
@@ -268,7 +287,7 @@
                     total[lines(half), span(face)] = summed
                     negative = jnp.minimum(summed, 0.0)
                     weighted = weighted + negative * negative * weights[0:1, span(face)]
-                running = project(half, pair, running)
+                running = multiply(half, pair, running)
             if turn + 1 == ITERS:
                 narrow = weighted[:, :lane]
                 for piece in range(1, per_face):
@@ -276,7 +295,9 @@
                 violated[lines(half), :] = narrow
                 if half + 1 == HALVES:
                     share_violation()
-            apply(turn + 1, half, running)
+            send_image(turn + 1, half, running)
+        if turn == 1:
+            prepare_weights()
         cheb_rho = rho_next
 
     for face in range(FACES):
@@ -401,7 +422,9 @@
             pltpu.VMEM((FACES, face_len, face_len), jnp.bfloat16),
             pltpu.VMEM((rows, columns), jnp.bfloat16),
             pltpu.VMEM((rows, columns), jnp.bfloat16),
-            pltpu.VMEM((rows, columns), jnp.bfloat16),
+            pltpu.VMEM((columns, rows), jnp.bfloat16),
+            pltpu.VMEM((columns, columns), jnp.bfloat16),
+            pltpu.VMEM((columns, columns), jnp.bfloat16),
             pltpu.VMEM((FACES, face_len, face_len), jnp.bfloat16),
             pltpu.VMEM((16, columns), jnp.float32),
             pltpu.VMEM((16, columns), jnp.float32),

time: 29.2 us -> 29.1 us (level)
  no operation moved by 1% of the time
where the time goes in v6:
time: 29.1 us; the launch traced here: 28.9 us
  Pallas kernels  27.6 us (95%)
  between operations  1.29 us (4%)
    pallas_call x1, Pallas kernels, local(): pl.pallas_call(functools.partial(kernel, n_space, n_bal), out_shape=(jax....  25.8 us
    pallas_call x1, Pallas kernels, local(): pl.pallas_call(finish, out_shape=(jax.ShapeDtypeStruct(field, jnp.float32...  1.79 us

profile of v6, /device:TPU:0, one launch (start us, length us, event | category | flops | bytes accessed | tf_op | source)
XLA Modules:
  0.0 28.9 jit_solution(17824642267591977794)
XLA Ops:
  1.3 25.8 %feti.1 = (f32[64,1024]{1,0:T(8,128)}, f32[64,1024]{1,0:T(8,128)}, f32[1,64]{1,0:T(1,128)}) custom-call(s32[1,4]{1,0:T(1,128)} %bitcast.15, s32[1,1]{1,0:T(1,128)S(6)} %copy.10.enrich_ref, s32[4,256]{1,0:T(4,128)} %bitcast.13, f32[1,1024]{1,0:T(1,128)} %bitcast.14, s32[1,128]{1,0:T(1,128)} %bitcast.16, f32[64,1024]{1,0:T(8,128)} %bitcast.10, ...), custom_call_target="tpu_custom_call" | custom-call | flops 2147483648 | bytes 2883584 | tf_op jit(solution)/shard_map/feti/pallas_call | solution.py:404
  27.1 1.8 %finish.1 = (f32[64,1024]{1,0:T(8,128)}, f32[64,1024]{1,0:T(8,128)}, f32[1,64]{1,0:T(1,128)}) custom-call(f32[64,1024]{1,0:T(8,128)} %get-tuple-element.9.solution_in, f32[64,1024]{1,0:T(8,128)} %get-tuple-element.10.residual_in, f32[1,64]{1,0:T(1,128)} %get-tuple-element.11.violation_in), custom_call_target="tpu_custom_call" | custom-call | tf_op jit(solution)/shard_map/finish/pallas_call | solution.py:460
